TPU v7x, 256 devices: a whole 4x4x8 slice. The times are simulated.
256 devices in a mesh: box: 64 (over y, z, core), chan: 4 (over x).
Axes of the slice: x: 4, y: 4, z: 8, core: 2. Of those that a mesh axis runs over, the one named last changes fastest.
Arguments:
- features: bfloat16 [64, 524288], P('chan', 'box'), may hold values from -6 to 6
- harmonics: bfloat16 [49, 524288], P(None, 'box'), may hold values from -0.75 to 0.75
- atom_leaf: int32 [524288], P('box'), may hold values from 0 to 127
- leaf_sources: int32 [8192, 189], P('box'), may hold values from -1 to 8191, as said below
- coarse_sources: int32 [128, 64], P('box'), may hold values from 0 to 127, as said below
- coarse_class: int32 [128, 64], P('box'), may hold values from 0 to 315
- child_to_parent: bfloat16 [8, 49, 49], replicated, may hold values from -0.3125 to 0.3125
- parent_to_child: bfloat16 [8, 49, 49], replicated, may hold values from -0.875 to 0.875
- leaf_transfer: bfloat16 [189, 49, 49], replicated, may hold values from -0.0625 to 0.0625
- coarse_transfer: bfloat16 [316, 49, 49], replicated, may hold values from -0.109375 to 0.109375
- mix_weight: bfloat16 [7, 64, 64], replicated, may hold values from -0.75 to 0.75
Outputs:
- field: bfloat16 [64, 524288], P('chan', 'box')
Inputs may be any that keep to these rules, and one draw needn't show every extreme that they name: `leaf_sources`: -1 marks an empty slot; every other entry is a leaf box other than the target itself, of the target's device's 128 leaves or of the 128 leaves just before or just after them; the outermost leaves of both neighbouring ranges occur wherever they exist. `coarse_sources`: the 64 sources of a coarse box are distinct coarse boxes other than itself.
All inputs are finite; a program needn't handle non-finite values.
Results may differ from a plain program's by a relative error of at most 0.015.
Values may be sent and summed in bfloat16 or wider, within the bound.
A program may use at most 64 MiB of HBM per device.

v0:
```python
import math

import jax
import jax.numpy as jnp
from jax import lax
from jax.sharding import PartitionSpec as P


def with_halo(array, sides, width):
    for axis, dim in sides:
        peers, length = (lax.axis_size(axis), array.shape[dim])
        up = [(i, (i + 1) % peers) for i in range(peers - 1)]
        down = [(j, i) for i, j in up]
        last = lax.slice_in_dim(array, length - width, length, axis=dim)
        first = lax.slice_in_dim(array, 0, width, axis=dim)
        before = lax.ppermute(last, axis, up)
        after = lax.ppermute(first, axis, down)
        array = jnp.concatenate([before, array, after], axis=dim)
    return array


def upward(children, table):
    coeffs, chans, count = children.shape
    grouped = children.reshape(coeffs, chans, count // 8, 8)
    result = jnp.einsum("oqk,kcmo->qcm", table, grouped, preferred_element_type=jnp.float32)
    return result.astype(jnp.bfloat16)


def downward(parents, table):
    coeffs, chans, count = parents.shape
    spread = jnp.einsum("oqk,kcp->qcpo", table, parents, preferred_element_type=jnp.float32)
    return spread.reshape(coeffs, chans, count * 8)


def on_device(
    features,
    harmonics,
    atom_leaf,
    leaf_sources,
    coarse_sources,
    coarse_class,
    child_to_parent,
    parent_to_child,
    leaf_transfer,
    coarse_transfer,
    mix_weight,
):
    coeffs = harmonics.shape[0]
    channels = features.shape[0]
    atom_count = features.shape[1]
    leaf_count = leaf_sources.shape[0]
    slot_count = leaf_sources.shape[1]
    coarse_count = coarse_sources.shape[0]
    coarse_slots = coarse_sources.shape[1]
    block_rows = math.gcd(atom_count, 1024)
    turn_count = atom_count // block_rows
    labels = lax.broadcasted_iota(jnp.int32, (block_rows, leaf_count), 1)

    def moments(block_index, running):
        begin = block_index * block_rows
        feat_block = lax.dynamic_slice_in_dim(features, begin, block_rows, 1).astype(jnp.float32)
        harm_block = lax.dynamic_slice_in_dim(harmonics, begin, block_rows, 1).astype(jnp.float32)
        leaf_block = lax.dynamic_slice_in_dim(atom_leaf, begin, block_rows, 0)
        products = (harm_block[:, None, :] * feat_block[None]).astype(jnp.bfloat16)
        products = products.reshape(coeffs * channels, block_rows)
        onehot = (leaf_block[:, None] == labels).astype(jnp.bfloat16)
        return running + jnp.dot(products, onehot, preferred_element_type=jnp.float32)

    summed = lax.fori_loop(
        0, turn_count, moments, jnp.zeros((coeffs * channels, leaf_count), jnp.float32)
    )
    leaf_multi = summed.astype(jnp.bfloat16).reshape(coeffs, channels, leaf_count)
    leaf_rows = leaf_multi.transpose(2, 1, 0)
    with_rims = with_halo(leaf_rows, (("box", 0),), leaf_count)
    padded = jnp.concatenate([with_rims, jnp.zeros((1, channels, coeffs), jnp.bfloat16)], 0)
    first_box = lax.axis_index("box") * leaf_count - leaf_count
    columns = jnp.where(leaf_sources >= 0, leaf_sources - first_box, 3 * leaf_count)

    def translate(block_index, running):
        chosen = lax.dynamic_slice_in_dim(columns, block_index * 7, 7, 1)
        picked = jnp.take(padded, chosen.T.reshape(-1), axis=0).reshape(
            7, leaf_count * channels, coeffs
        )
        matrices = lax.dynamic_slice_in_dim(leaf_transfer, block_index * 7, 7, 0)
        return running + jnp.einsum(
            "jrk,jqk->rq", picked, matrices, preferred_element_type=jnp.float32
        )

    far_rows = lax.fori_loop(
        0, slot_count // 7, translate, jnp.zeros((leaf_count * channels, coeffs), jnp.float32)
    )
    far_leaf = far_rows.reshape(leaf_count, channels, coeffs).transpose(2, 1, 0)
    mid_multi = upward(leaf_multi, child_to_parent)
    coarse_multi = upward(mid_multi, child_to_parent)
    coarse_rows = coarse_multi.transpose(2, 1, 0)
    matrices = jnp.take(coarse_transfer, coarse_class.reshape(-1), axis=0).reshape(
        coarse_count, coarse_slots, coeffs, coeffs
    )
    piece_rows = lax.all_gather(coarse_rows, "box", axis=0, tiled=True)
    piece_width = piece_rows.shape[0]
    inside = (coarse_sources >= 0) & (coarse_sources < piece_width)
    clipped = jnp.clip(coarse_sources, 0, piece_width - 1).reshape(-1)
    picked = jnp.take(piece_rows, clipped, axis=0).reshape(
        coarse_count, coarse_slots, channels, coeffs
    )
    picked = jnp.where(inside[:, :, None, None], picked, jnp.zeros_like(picked))
    coarse_sum = jnp.einsum("tjqk,tjck->qct", matrices, picked, preferred_element_type=jnp.float32)
    coarse_local = coarse_sum.astype(jnp.bfloat16)
    mid_local = downward(coarse_local, parent_to_child).astype(jnp.bfloat16)
    leaf_local = (downward(mid_local, parent_to_child) + far_leaf).astype(jnp.bfloat16)
    group_start = lax.axis_index("chan") * channels
    degree_count = mix_weight.shape[0]
    pieces = []
    gathered_local = lax.all_gather(leaf_local, "chan", axis=1, tiled=True)
    for degree in range(degree_count):
        row_block = gathered_local[degree * degree : (degree + 1) * (degree + 1)]
        weight = lax.dynamic_slice_in_dim(mix_weight[degree], group_start, channels, 0)
        pieces.append(
            jnp.einsum("xc,kcb->kxb", weight, row_block, preferred_element_type=jnp.float32)
        )
    mixed = jnp.concatenate(pieces, 0).astype(jnp.bfloat16)
    flattened = mixed.reshape(coeffs * channels, leaf_count)
    leaf_labels = lax.broadcasted_iota(jnp.int32, (leaf_count, block_rows), 0)

    def evaluate(block_index, outputs):
        begin = block_index * block_rows
        harm_block = lax.dynamic_slice_in_dim(harmonics, begin, block_rows, 1).astype(jnp.float32)
        leaf_block = lax.dynamic_slice_in_dim(atom_leaf, begin, block_rows, 0)
        onehot = (leaf_labels == leaf_block[None, :]).astype(jnp.bfloat16)
        selected = jnp.dot(flattened, onehot, preferred_element_type=jnp.float32).reshape(
            coeffs, channels, block_rows
        )
        result = jnp.sum(harm_block[:, None, :] * selected, 0).astype(jnp.bfloat16)
        return lax.dynamic_update_slice_in_dim(outputs, result, begin, 1)

    return lax.fori_loop(0, turn_count, evaluate, jnp.zeros((channels, atom_count), jnp.bfloat16))


def solution(mesh):
    placed = (
        P("chan", "box"),
        P(None, "box"),
        P("box"),
        P("box", None),
        P("box", None),
        P("box", None),
        P(),
        P(),
        P(),
        P(),
        P(),
    )
    return jax.shard_map(
        on_device, mesh=mesh, in_specs=placed, out_specs=P("chan", "box"), check_vma=False
    )
```

profile of v0, /device:TPU:1, one launch (start us, length us, event | category | flops | bytes accessed | tf_op | source)
XLA Modules:
  0.0 436.7 jit_solution(5056000769091387244)
XLA Ops:
  0.0 28.4 %while.43 = (s32[]{:T(128)}, f32[784,128]{1,0:T(8,128)S(1)}, bf16[49,8192]{1,0:T(8,128)(2,1)}, bf16[16,8192]{1,0:T(8,128)(2,1)}, s32[8192]{0:T(1024)}, /*index=5*/s32[]{:T(128)}, s32[]{:T(128)}, s32[]{:T(128)}, s32[]{:T(128)}) while((s32[]{:T(128)}, f32[784,128]{1,0:T(8,128)S(1)}, bf16[49,8192]{1,0:T(8,128)(2,1)}, ...), condition=%wide.region_1.0_spmd.clone, body=%wide.region_0.0_spmd.clone.sunk | while | flops 207524864 | bytes 4692129 | solution.py:69
  28.4 4.9 %collective-permute-start = (bf16[128,16,49]{0,1,2:T(8,128)(2,1)S(1)}, bf16[128,16,49]{0,1,2:T(8,128)(2,1)S(1)}, u32[]{:S(2)}, u32[]{:S(2)}) collective-permute-start(bf16[128,16,49]{0,1,2:T(8,128)(2,1)S(1)} %bitcast.182), channel_id=1, source_target_pairs={{0,4},{4,8},{8,12},{12,16},{16,20},{20,24},{24,28},{28,32},{32,36}... | collective-permute-start | bytes 602120 | tf_op jit(solution)/shard_map/ppermute | solution.py:16
  35.6 5.4 %copy.48 = bf16[189,49,49]{2,1,0:T(8,128)(2,1)} copy(bf16[189,49,49]{0,2,1:T(8,128)(2,1)} %param.25) | data formatting | bytes 1815156
  43.1 53.9 %all_gather.6 = bf16[128,16,49]{2,1,0:T(8,128)(2,1)S(1)} all-gather(bf16[2,16,49]{2,1,0:T(8,128)(2,1)S(1)} %fusion.41), channel_id=1, replica_groups=mesh['box'=64,'chan'=4] {'box'}, dimensions={0}, use_global_device_ids=true | all-gather | bytes 203840 | tf_op jit(solution)/shard_map/all_gather | solution.py:99
  97.1 11.1 %copy.42 = bf16[316,49,49]{2,1,0:T(8,128)(2,1)} copy(bf16[316,49,49]{0,2,1:T(8,128)(2,1)} %param.26) | data formatting | bytes 3034864 | tf_op args[9]
  117.1 281.1 %while.44 = (s32[]{:T(128)}, f32[2048,49]{0,1:T(8,128)}, s32[128,189]{0,1:T(8,128)S(1)}, bf16[385,16,49]{2,1,0:T(8,128)(2,1)S(1)}, bf16[189,49,49]{2,1,0:T(8,128...) while((s32[]{:T(128)}, f32[2048,49]{0,1:T(8,128)}, s32[128,189]{0,1:T(8,128)S(1)}, ...), condition=%wide.region_3.4_spmd.clone, body=%wide.region_2.3_spmd.clone.sunk | while | flops 69753736 | bytes 8073633 | solution.py:89
  117.1 4.0 gather_fusion
  127.4 4.0 gather_fusion
  137.8 4.0 gather_fusion
  148.2 4.0 gather_fusion
  152.2 3.5 copy.85
  158.6 4.0 gather_fusion
  169.0 4.0 gather_fusion
  173.1 3.5 copy.85
  179.4 4.0 gather_fusion
  183.5 3.5 copy.85
  189.9 4.0 gather_fusion
  193.9 3.5 copy.85
  200.3 4.0 gather_fusion
  210.7 4.0 gather_fusion
  214.7 3.5 copy.85
  221.1 4.0 gather_fusion
  231.5 4.0 gather_fusion
  241.9 4.0 gather_fusion
  246.0 3.5 copy.85
  252.3 4.0 gather_fusion
  256.4 3.5 copy.85
  262.8 4.0 gather_fusion
  273.2 4.0 gather_fusion
  277.2 3.5 copy.85
  283.6 4.0 gather_fusion
  287.6 3.5 copy.85
  294.0 4.0 gather_fusion
  304.4 4.0 gather_fusion
  314.8 4.0 gather_fusion
  318.9 3.5 copy.85
  325.3 4.0 gather_fusion
  335.7 4.0 gather_fusion
  346.1 4.0 gather_fusion
  350.1 3.5 copy.85
  356.5 4.0 gather_fusion
  360.5 3.5 copy.85
  366.9 4.0 gather_fusion
  370.9 3.5 copy.85
  377.3 4.0 gather_fusion
  387.7 4.0 gather_fusion
  400.2 12.1 %all_gather.7 = bf16[49,64,128]{2,1,0:T(8,128)(2,1)S(1)} all-gather(bf16[49,16,128]{2,1,0:T(8,128)(2,1)S(1)} %fusion.56), channel_id=1, replica_groups=mesh['box'=64,'chan'=4] {'chan'}, dimensions={1}, use_global_device_ids=true | all-gather | bytes 1003520 | tf_op jit(solution)/shard_map/all_gather | solution.py:114
  413.3 22.7 %while.42 = (s32[]{:T(128)}, bf16[16,8192]{1,0:T(8,128)(2,1)S(1)}, bf16[49,8192]{1,0:T(8,128)(2,1)}, s32[8192]{0:T(1024)}, bf16[784,128]{1,0:T(8,128)(2,1)S(1)},...) while((s32[]{:T(128)}, bf16[16,8192]{1,0:T(8,128)(2,1)S(1)}, bf16[49,8192]{1,0:T(8,128)(2,1)}, ...), condition=%wide.region_6.7_spmd.clone, body=%wide.region_4.6_spmd.clone.sunk | while | flops 207291392 | bytes 7235735 | solution.py:136
  (339 shorter events, 192.8 us)
Async XLA Ops:
  0.0 35.5 %copy-start.6 = (s32[2,64]{1,0:T(2,128)S(1)}, s32[2,64]{1,0:T(2,128)}, u32[]{:S(2)}) copy-start(s32[2,64]{1,0:T(2,128)} %param.21) | copy-start | bytes 1540
  0.0 35.5 %copy-start.7 = (s32[2,64]{1,0:T(2,128)S(1)}, s32[2,64]{1,0:T(2,128)}, u32[]{:S(2)}) copy-start(s32[2,64]{1,0:T(2,128)} %param.22) | copy-start | bytes 1540
  28.4 86.4 %collective-permute-start = (bf16[128,16,49]{0,1,2:T(8,128)(2,1)S(1)}, bf16[128,16,49]{0,1,2:T(8,128)(2,1)S(1)}, u32[]{:S(2)}, u32[]{:S(2)}) collective-permute-start(bf16[128,16,49]{0,1,2:T(8,128)(2,1)S(1)} %bitcast.182), channel_id=1, source_target_pairs={{0,4},{4,8},{8,12},{12,16},{16,20},{20,24},{24,28},{28,32},{32,36}... | collective-permute-start | bytes 602120 | tf_op jit(solution)/shard_map/ppermute | solution.py:16
  33.4 81.5 %collective-permute-start.1 = (bf16[128,16,49]{0,1,2:T(8,128)(2,1)S(1)}, bf16[128,16,49]{0,1,2:T(8,128)(2,1)S(1)}, u32[]{:S(2)}, u32[]{:S(2)}) collective-permute-start(bf16[128,16,49]{0,1,2:T(8,128)(2,1)S(1)} %bitcast.183), channel_id=1, source_target_pairs={{4,0},{8,4},{12,8},{16,12},{20,16},{24,20},{28,24},{32,28},{36,32}... | collective-permute-start | bytes 602120 | tf_op jit(solution)/shard_map/ppermute | solution.py:17
  41.1 1.2 copy-start.1
  108.9 3.3 copy-start.3
  113.3 1.5 copy-start.5
  113.3 1.5 copy-start.4
  398.1 2.0 copy-start
  436.0 0.7 copy-start.2
where the time goes:
time: 442 us; the launch traced here: 437 us
  local copies, waits for them, and re-layouts  256 us (58%)
  matrix products  76 us (17%)
  blocking collectives  66 us (15%)
  other arithmetic  29.7 us (7%)
  starting transfers between devices  6.86 us (2%)
    gather x54, local copies, waits for them, and re-layouts, translate(): jnp.take(padded, chosen.T.reshape(-1), axis=0)  204 us
    dot_general x27, matrix products, translate(): jnp.einsum('jrk,jqk->rq', picked, matrices, preferred_element_type=jnp.fl...  61.8 us
    all_gather x1, blocking collectives, on_device(): piece_rows = lax.all_gather(coarse_rows, 'box', axis=0, tiled=True)  53.9 us
    unnamed x19, local copies, waits for them, and re-layouts  19.1 us
    broadcast_in_dim x54, local copies, waits for them, and re-layouts, translate(): jnp.take(padded, chosen.T.reshape(-1), axis=0)  13 us
    all_gather x1, blocking collectives, on_device(): gathered_local = lax.all_gather(leaf_local, 'chan', axis=1, tiled=True)  12.1 us
  transfers between devices with their start and end apart: 2, of which 0 were waited for; matrix products, arithmetic and copies ran while one was open for 6% of the time, Pallas kernels for 0%

commit v1 on v0

v1 whole, which is shorter than its diff:
```python
import jax
import jax.numpy as jnp
import numpy as np
from jax import lax
from jax.experimental import pallas as pl
from jax.experimental.pallas import tpu as pltpu
from jax.sharding import PartitionSpec as P

F32 = jnp.float32
BF16 = jnp.bfloat16
K = 49
KP = 64
CH = 16
CP = 8
LB = 128
ATOMS = 8192
SLOTS = 189
NT = (((1,), (1,)), ((), ()))
VMEM = pl.BlockSpec(memory_space=pltpu.VMEM)
SMEM = pl.BlockSpec(memory_space=pltpu.SMEM)
DEGREE = np.array([int(np.sqrt(k)) for k in range(K)])


def dot_nt(a, b):
    return lax.dot_general(a, b, NT, preferred_element_type=F32)


def twice(block):
    wide = jnp.concatenate([block.astype(F32), jnp.zeros((K, 128 - K), F32)], 1)
    tall = jnp.concatenate([wide, jnp.zeros((KP - K, 128), F32)], 0)
    return jnp.concatenate([tall, pltpu.roll(tall, KP, 1)], 0).astype(BF16)


def moments_kernel(feat, harm, leaf, up, tiles_out, coarse_out, hpad, acc, rows32, mid32):
    step = 512
    hpad[...] = jnp.concatenate([harm[...].astype(F32), jnp.zeros((KP - K, ATOMS), F32)], 0).astype(BF16)
    acc[...] = jnp.zeros_like(acc)

    def turn(i, carry):
        at = pl.ds(pl.multiple_of(i * step, step), step)
        onehot = jnp.where(
            leaf[:, at] == lax.broadcasted_iota(jnp.int32, (LB, step), 0), 1.0, 0.0
        ).astype(BF16)
        h = hpad[:, at]
        f = feat[:, at]
        for group in range(4):
            products = jnp.concatenate([h * f[4 * group + c : 4 * group + c + 1] for c in range(4)], 0)
            cols = slice(group * 256, group * 256 + 256)
            acc[:, cols] += dot_nt(onehot, products)
        return carry

    lax.fori_loop(0, ATOMS // step, turn, 0)
    for pair in range(CP):
        part = acc[:, pair * 128 : pair * 128 + 128].astype(BF16).astype(F32)
        rows32[pl.ds(pair, LB, stride=CP), :] = part
    tiles = rows32[...].astype(BF16)
    tiles_out[...] = tiles
    tables = [twice(up[o]) for o in range(8)]
    by_child = rows32[...].reshape(16, 8, CP, 128)
    mid = jnp.zeros((128, 128), F32)
    for o in range(8):
        mid += dot_nt(by_child[:, o].reshape(128, 128).astype(BF16), tables[o])
    mid32[...] = mid.astype(BF16).astype(F32)
    mids = mid32[...].reshape(2, 8, CP, 128)
    coarse = jnp.zeros((16, 128), F32)
    for o in range(8):
        coarse += dot_nt(mids[:, o].reshape(16, 128).astype(BF16), tables[o])
    coarse_out[...] = coarse.astype(BF16)


def far_kernel(
    index, csource, cclass, before, own, after, coarse, transfer, ctransfer, down,
    out, table, weights, call32, far32, local32, mid32,
):
    for place, block in enumerate((before, own, after)):
        table[place * 1024 : place * 1024 + 1024, :] = block[...].astype(F32)
    table[3072:3080, :] = jnp.zeros((8, 128), F32)
    call32[...] = coarse[...].astype(F32)

    def build(i, carry):
        for r in range(9):
            j = i * 9 + r
            weights[j] = twice(transfer[j])
        return carry

    lax.fori_loop(0, 21, build, 0)
    for j in range(SLOTS, 192):
        weights[j] = jnp.zeros((128, 128), BF16)

    def block(tb, carry):
        def chunk(jc, acc):
            def pick(jj, t):
                row = index[tb * 6 + jc, jj % 8, (jj // 8) * 32 + t]
                return table[pl.ds(pl.multiple_of(row, 8), 8), :]

            parts = []
            for jj in range(32):
                pairs = [
                    jnp.concatenate([pick(jj, t), pick(jj, t + 1)], 0).astype(BF16) for t in range(0, 32, 2)
                ]
                parts.append(jnp.concatenate(pairs, 0))
            lhs = jnp.concatenate(parts, 1)
            rhs = jnp.concatenate([weights[jc * 32 + jj] for jj in range(32)], 1)
            return acc + dot_nt(lhs, rhs)

        total = lax.fori_loop(0, 6, chunk, jnp.zeros((256, 128), F32))
        far32[pl.ds(pl.multiple_of(tb * 256, 256), 256), :] = total
        return carry

    lax.fori_loop(0, 4, block, 0)

    def coarse_target(target):
        def slots(i, acc):
            for r in range(8):
                j = target * 64 + i * 8 + r
                x = call32[pl.ds(pl.multiple_of(csource[j] * 8, 8), 8), :]
                both = jnp.concatenate([x, pltpu.roll(x, KP, 1)], 0)[:, :K].astype(BF16)
                acc = acc + dot_nt(both, ctransfer[cclass[j]])
            return acc

        acc = lax.fori_loop(0, 8, slots, jnp.zeros((16, K), F32))
        wide = jnp.concatenate([acc, jnp.zeros((16, 128 - K), F32)], 1)
        return wide[:8] + pltpu.roll(wide[8:], KP, 1)

    coarse_local = jnp.concatenate([coarse_target(0), coarse_target(1)], 0).astype(BF16)
    tables = [twice(down[o]) for o in range(8)]
    for o in range(8):
        mid = dot_nt(coarse_local, tables[o])
        mid32[o * 8 : o * 8 + 8, :] = mid[:8]
        mid32[64 + o * 8 : 64 + o * 8 + 8, :] = mid[8:]
    mids = mid32[...].astype(BF16)
    for o in range(8):
        local32[:, o] = dot_nt(mids, tables[o]).reshape(16, CP, 128)
    far32[...] += local32[...].reshape(1024, 128)
    for pair in range(CP):
        out[:, pair * 128 : pair * 128 + 128] = far32[pl.ds(pair, LB, stride=CP), :].astype(BF16)


def field_kernel(harm, leaf, local, wide_mix, out, acc, mixed):
    acc[...] = jnp.zeros_like(acc)
    for dev in range(4):
        def mix(i, carry):
            cols = pl.ds(pl.multiple_of(i * 512, 512), 512)
            weight = wide_mix[:, pl.ds(pl.multiple_of(dev * 1024 + i * 512, 512), 512)].astype(F32)
            lane = lax.rem(lax.broadcasted_iota(jnp.int32, (16, 512), 1), KP)
            lhs = jnp.concatenate([jnp.where(lane == q, weight, 0.0).astype(BF16) for q in range(K)], 0)
            acc[...] += dot_nt(lhs, local[dev, :, cols])
            return carry

        lax.fori_loop(0, 2, mix, 0)
    mixed[...] = acc[...].astype(BF16)
    step = 256

    def turn(i, carry):
        at = pl.ds(pl.multiple_of(i * step, step), step)
        onehot = jnp.where(
            leaf[:, at] == lax.broadcasted_iota(jnp.int32, (LB, step), 0), 1.0, 0.0
        ).astype(BF16)
        picked = jnp.dot(mixed[...], onehot, preferred_element_type=F32)
        h = harm[:, at].astype(F32)
        total = jnp.zeros((CH, step), F32)
        for q in range(K):
            total += h[q : q + 1] * picked[q * 16 : q * 16 + 16]
        out[:, at] = total.astype(BF16)
        return carry

    lax.fori_loop(0, ATOMS // step, turn, 0)


def on_device(
    features, harmonics, atom_leaf, leaf_sources, coarse_sources, coarse_class,
    child_to_parent, parent_to_child, leaf_transfer, coarse_transfer, mix_weight,
):
    params = pltpu.CompilerParams(vmem_limit_bytes=60 << 20)
    leaf_row = atom_leaf.reshape(1, ATOMS)
    tiles, coarse = pl.pallas_call(
        moments_kernel,
        out_shape=(jax.ShapeDtypeStruct((1024, 128), BF16), jax.ShapeDtypeStruct((16, 128), BF16)),
        in_specs=[VMEM] * 4,
        out_specs=(VMEM, VMEM),
        scratch_shapes=[
            pltpu.VMEM((KP, ATOMS), BF16),
            pltpu.VMEM((LB, 1024), F32),
            pltpu.VMEM((1024, 128), F32),
            pltpu.VMEM((128, 128), F32),
        ],
        compiler_params=params,
        name="moments",
    )(features, harmonics, leaf_row, child_to_parent)

    peers = lax.axis_size("box")
    up = [(i, i + 1) for i in range(peers - 1)]
    down = [(i + 1, i) for i in range(peers - 1)]
    before = lax.ppermute(tiles, "box", up)
    after = lax.ppermute(tiles, "box", down)
    coarse_all = lax.all_gather(coarse, "box", axis=0, tiled=True)

    first = lax.axis_index("box") * LB - LB
    index = jnp.where(leaf_sources >= 0, (leaf_sources - first) * 8, 3072)
    index = jnp.pad(index, ((0, 0), (0, 3)), constant_values=3072)
    index = index.reshape(4, 32, 6, 4, 8).transpose(0, 2, 4, 3, 1).reshape(24, 8, 128)

    local = pl.pallas_call(
        far_kernel,
        out_shape=jax.ShapeDtypeStruct((LB, 1024), BF16),
        in_specs=[SMEM] * 3 + [VMEM] * 7,
        out_specs=VMEM,
        scratch_shapes=[
            pltpu.VMEM((3080, 128), F32),
            pltpu.VMEM((192, 128, 128), BF16),
            pltpu.VMEM((1024, 128), F32),
            pltpu.VMEM((1024, 128), F32),
            pltpu.VMEM((16, 8, CP, 128), F32),
            pltpu.VMEM((128, 128), F32),
        ],
        compiler_params=params,
        name="far",
    )(
        index, coarse_sources.reshape(-1), coarse_class.reshape(-1), before, tiles, after,
        coarse_all, leaf_transfer, coarse_transfer, parent_to_child,
    )
    local_all = lax.all_gather(local, "chan", axis=0)

    start = lax.axis_index("chan") * CH
    mine = lax.dynamic_slice_in_dim(mix_weight, start, CH, 1)
    wide = jnp.pad(mine[DEGREE], ((0, KP - K), (0, 0), (0, 0)))
    wide = wide.transpose(1, 2, 0).reshape(CH, 64 * KP)
    return pl.pallas_call(
        field_kernel,
        out_shape=jax.ShapeDtypeStruct((CH, ATOMS), BF16),
        in_specs=[VMEM] * 4,
        out_specs=VMEM,
        scratch_shapes=[pltpu.VMEM((K * 16, 128), F32), pltpu.VMEM((K * 16, 128), BF16)],
        compiler_params=params,
        name="field",
    )(harmonics, leaf_row, local_all, wide)


def solution(mesh):
    placed = (
        P("chan", "box"), P(None, "box"), P("box"), P("box", None), P("box", None), P("box", None),
        P(), P(), P(), P(), P(),
    )
    return jax.shard_map(
        on_device, mesh=mesh, in_specs=placed, out_specs=P("chan", "box"), check_vma=False
    )
```

time: 442 us -> 179 us (0.40); the launches traced: 437 us -> 179 us
  local copies, waits for them, and re-layouts: 256 us -> 24.9 us
  matrix products: 76 us -> 0 us
  Pallas kernels: 0 us -> 59.5 us
  other arithmetic: 29.7 us -> 0.92 us
  waiting for transfers between devices: 0.01 us -> 22.2 us
  blocking collectives: 66 us -> 51 us
  between operations: 0.28 us -> 13.5 us
    gather x56 -> x1, local copies, waits for them, and re-layouts: 208 us -> 0.61 us  [on_device(): wide = jnp.pad(mine[DEGREE], ((0, KP - K), (0, 0), (0, 0)))]
    dot_general x54 -> x0, matrix products: 76 us -> none  [the longest x27 61.8 us: translate(): jnp.einsum('jrk,jqk->rq', picked, matrices, preferred_element_type=jnp.fl...]
    pallas_call x0 -> x3, Pallas kernels: none -> 59.5 us  [the longest x1 34.5 us: on_device(): pl.pallas_call(far_kernel, out_shape=jax.ShapeDtypeStruct((LB, 1024), BF1...]
    convert_element_type x34 -> x0, other arithmetic: 23.6 us -> none  [the longest x8 7.38 us: evaluate(): lax.dynamic_slice_in_dim(harmonics, begin, block_rows, 1)]
    all_gather x0 -> x1, waiting for transfers between devices: none -> 22.1 us  [on_device(): local_all = lax.all_gather(local, 'chan', axis=0)]
    all_gather x2 -> x1, blocking collectives: 66 us -> 51 us  [on_device(): coarse_all = lax.all_gather(coarse, 'box', axis=0, tiled=True)]
    broadcast_in_dim x55 -> x0, local copies, waits for them, and re-layouts: 13 us -> none  [the longest x54 13 us: translate(): jnp.take(padded, chosen.T.reshape(-1), axis=0)]
    dynamic_slice x16 -> x1, local copies, waits for them, and re-layouts: 11.1 us -> 0.01 us  [on_device(): mine = lax.dynamic_slice_in_dim(mix_weight, start, CH, 1)]
  transfers between devices with their start and end apart: 2 -> 3, of which waited for: 0 -> 1; matrix products, arithmetic and copies ran while one was open for 6% -> 13% of each run, Pallas kernels for 0% -> 0%
where the time goes in v1:
time: 179 us
  Pallas kernels  59.5 us (33%)
  blocking collectives  51 us (28%)
  local copies, waits for them, and re-layouts  24.9 us (14%)
  waiting for transfers between devices  22.2 us (12%)
  between operations  13.5 us (8%)
  starting transfers between devices  6.84 us (4%)
    all_gather x1, blocking collectives, on_device(): coarse_all = lax.all_gather(coarse, 'box', axis=0, tiled=True)  51 us
    pallas_call x1, Pallas kernels, on_device(): pl.pallas_call(far_kernel, out_shape=jax.ShapeDtypeStruct((LB, 1024), BF1...  34.5 us
    all_gather x1, waiting for transfers between devices, on_device(): local_all = lax.all_gather(local, 'chan', axis=0)  22.1 us
    unnamed x22, local copies, waits for them, and re-layouts  20.5 us
    pallas_call x1, Pallas kernels, on_device(): pl.pallas_call(field_kernel, out_shape=jax.ShapeDtypeStruct((CH, ATOMS),...  14.5 us
    pallas_call x1, Pallas kernels, on_device(): pl.pallas_call(moments_kernel, out_shape=(jax.ShapeDtypeStruct((1024, 128...  10.6 us
    ppermute x1, starting transfers between devices, on_device(): before = lax.ppermute(tiles, 'box', up)  4.92 us
  transfers between devices with their start and end apart: 3, of which 1 were waited for; matrix products, arithmetic and copies ran while one was open for 13% of the time, Pallas kernels for 0%

profile of v1, /device:TPU:1, one launch (start us, length us, event | category | flops | bytes accessed | tf_op | source)
XLA Modules:
  0.0 178.7 jit_solution(6125505118415602326)
XLA Ops:
  6.5 0.0 copy-start
  6.5 0.0 copy-start.1
  6.5 0.0 all-gather.3.cloned.1.call-start
  6.5 1.7 copy.15.up
  8.2 10.6 %moments.1 = (bf16[1024,128]{1,0:T(8,128)(2,1)}, bf16[16,128]{1,0:T(8,128)(2,1)}) custom-call(bf16[16,8192]{1,0:T(8,128)(2,1)} %feat.1, bf16[49,8192]{1,0:T(8,128)(2,1)} %harm.3, s32[1,8192]{1,0:T(1,128)} %bitcast.11, bf16[8,49,49]{2,1,0:T(8,128)(2,1)} %copy.15.up), custom_call_target="tpu_custom_call" | custom-call | tf_op jit(solution)/shard_map/moments/pallas_call | solution.py:176
  18.8 4.9 %collective-permute-start = (bf16[1024,128]{1,0:T(8,128)(2,1)}, bf16[1024,128]{1,0:T(8,128)(2,1)S(1)}, u32[]{:S(2)}, u32[]{:S(2)}) collective-permute-start(bf16[1024,128]{1,0:T(8,128)(2,1)} %get-tuple-element.7.own), channel_id=1, source_target_pairs={{0,4},{4,8},{8,12},{12,16},{16,20},{20,24},{24,28},{28,32},{32,36}... | collective-permute-start | bytes 786440 | tf_op jit(solution)/shard_map/ppermute | solution.py:194
  23.7 1.9 %collective-permute-start.1 = (bf16[1024,128]{1,0:T(8,128)(2,1)}, bf16[1024,128]{1,0:T(8,128)(2,1)S(1)}, u32[]{:S(2)}, u32[]{:S(2)}) collective-permute-start(bf16[1024,128]{1,0:T(8,128)(2,1)} %get-tuple-element.7.own), channel_id=1, source_target_pairs={{4,0},{8,4},{12,8},{16,12},{20,16},{24,20},{28,24},{32,28},{36,32}... | collective-permute-start | bytes 786440 | tf_op jit(solution)/shard_map/ppermute | solution.py:195
  25.7 0.9 multiply_select_fusion
  26.6 0.2 reshape.19
  26.8 0.3 copy.21
  27.1 0.8 reshape.20.index
  27.9 0.0 copy-done.1
  27.9 11.2 %copy.17.ctransfer = bf16[316,49,49]{2,1,0:T(8,128)(2,1)} copy(bf16[316,49,49]{0,2,1:T(8,128)(2,1)S(1)} %copy-done.1) | data formatting | bytes 3034864 | tf_op args[9]
  39.1 0.0 copy-start.4
  39.1 0.0 copy-start.7
  39.1 0.0 copy-start.8
  39.1 0.0 copy-start.5
  39.1 5.5 %copy.16.transfer = bf16[189,49,49]{2,1,0:T(8,128)(2,1)} copy(bf16[189,49,49]{0,2,1:T(8,128)(2,1)} %param.21) | data formatting | bytes 1815156 | tf_op args[8]
  44.6 0.0 copy-done.4
  44.6 0.7 copy.18.down
  45.3 0.0 copy-done.7
  45.3 0.6 reshape.21.csource
  45.9 0.0 copy-done.8
  45.9 0.6 reshape.22.cclass
  46.5 0.0 copy-done.5
  46.5 51.0 %all_gather.9.coarse = bf16[1024,128]{1,0:T(8,128)(2,1)} all-gather(bf16[16,128]{1,0:T(8,128)(2,1)S(1)} %copy-done.5), channel_id=1, replica_groups=mesh['box'=64,'chan'=4] {'box'}, dimensions={0}, use_global_device_ids=true | all-gather | bytes 266240 | tf_op jit(solution)/shard_map/all_gather | solution.py:196
  97.5 0.0 copy-start.6
  97.5 0.0 collective-permute-done.before
  97.5 0.0 copy-start.2
  97.5 0.0 collective-permute-done.1.after
  97.5 0.7 copy-done.2
  98.2 0.0 copy-start.3
  98.2 0.7 copy-done.3
  98.9 34.5 %far.1 = bf16[128,1024]{1,0:T(8,128)(2,1)} custom-call(s32[24,8,128]{2,1,0:T(8,128)} %reshape.20.index, s32[128]{0:T(128)} %reshape.21.csource, s32[128]{0:T(128)} %reshape.22.cclass, bf16[1024,128]{1,0:T(8,128)(2,1)} %copy-done.2, bf16[1024,128]{1,0:T(8,128)(2,1)} %get-tuple-element.7.own, bf16[1024,128]{1,0:T(8,128)(2,1)} %copy-done.3, ...), custom_call_target="tpu_custom_call" | custom-call | tf_op jit(solution)/shard_map/far/pallas_call | solution.py:203
  133.3 0.0 all-gather.3.cloned.1.call-update
  133.3 0.0 copy-done.6
  133.4 0.0 copy-done
  133.4 0.6 gather_fusion
  134.1 0.3 copy.19
  134.3 0.9 reshape.23.wide_mix
  135.3 22.1 %all-gather.3.cloned.1.call-done = bf16[512,1024]{1,0:T(8,128)(2,1)} async-done(((bf16[128,1024]{1,0:T(8,128)(2,1)}), bf16[512,1024]{1,0:T(8,128)(2,1)}) %all-gather.3.cloned.1.call-update) | async-done | bytes 1048592 | tf_op jit(solution)/shard_map/all_gather | solution.py:222
  157.4 14.5 %field.1 = bf16[16,8192]{1,0:T(8,128)(2,1)} custom-call(bf16[49,8192]{1,0:T(8,128)(2,1)} %harm.3, s32[1,8192]{1,0:T(1,128)} %bitcast.12, bf16[4,128,1024]{2,1,0:T(8,128)(2,1)} %bitcast.10, bf16[16,4096]{1,0:T(8,128)(2,1)} %reshape.23.wide_mix), custom_call_target="tpu_custom_call" | custom-call | tf_op jit(solution)/shard_map/field/pallas_call | solution.py:228
  (4 shorter events, 0.1 us)
Async XLA Ops:
  6.5 126.8 %copy-start = (bf16[7,64,64]{2,1,0:T(8,128)(2,1)S(1)}, bf16[7,64,64]{2,1,0:T(8,128)(2,1)}, u32[]{:S(2)}) copy-start(bf16[7,64,64]{2,1,0:T(8,128)(2,1)} %param.23) | copy-start | bytes 172036
  6.5 21.4 %copy-start.1 = (bf16[316,49,49]{0,2,1:T(8,128)(2,1)S(1)}, bf16[316,49,49]{0,2,1:T(8,128)(2,1)}, u32[]{:S(2)}) copy-start(bf16[316,49,49]{0,2,1:T(8,128)(2,1)} %param.22) | copy-start | bytes 4552300
  6.5 150.9 %all-gather.3.cloned.1.call-start = ((), (), s32[]{:S(2)}) async-start(), calls=%async_computation | async-start | bytes 1310720 | tf_op jit(solution)/shard_map/all_gather | solution.py:222
  18.8 78.7 %collective-permute-start = (bf16[1024,128]{1,0:T(8,128)(2,1)}, bf16[1024,128]{1,0:T(8,128)(2,1)S(1)}, u32[]{:S(2)}, u32[]{:S(2)}) collective-permute-start(bf16[1024,128]{1,0:T(8,128)(2,1)} %get-tuple-element.7.own), channel_id=1, source_target_pairs={{0,4},{4,8},{8,12},{12,16},{16,20},{20,24},{24,28},{28,32},{32,36}... | collective-permute-start | bytes 786440 | tf_op jit(solution)/shard_map/ppermute | solution.py:194
  23.7 73.7 %collective-permute-start.1 = (bf16[1024,128]{1,0:T(8,128)(2,1)}, bf16[1024,128]{1,0:T(8,128)(2,1)S(1)}, u32[]{:S(2)}, u32[]{:S(2)}) collective-permute-start(bf16[1024,128]{1,0:T(8,128)(2,1)} %get-tuple-element.7.own), channel_id=1, source_target_pairs={{4,0},{8,4},{12,8},{16,12},{20,16},{24,20},{28,24},{32,28},{36,32}... | collective-permute-start | bytes 786440 | tf_op jit(solution)/shard_map/ppermute | solution.py:195
  39.1 5.5 %copy-start.4 = (bf16[8,49,49]{2,0,1:T(8,128)(2,1)S(1)}, bf16[8,49,49]{2,0,1:T(8,128)(2,1)}, u32[]{:S(2)}) copy-start(bf16[8,49,49]{2,0,1:T(8,128)(2,1)} %param.20) | copy-start | bytes 115252
  39.1 6.2 %copy-start.7 = (s32[2,64]{1,0:T(2,128)S(1)}, s32[2,64]{1,0:T(2,128)}, u32[]{:S(2)}) copy-start(s32[2,64]{1,0:T(2,128)} %param.17) | copy-start | bytes 1540
  39.1 6.8 %copy-start.8 = (s32[2,64]{1,0:T(2,128)S(1)}, s32[2,64]{1,0:T(2,128)}, u32[]{:S(2)}) copy-start(s32[2,64]{1,0:T(2,128)} %param.18) | copy-start | bytes 1540
  39.1 7.4 %copy-start.5 = (bf16[16,128]{1,0:T(8,128)(2,1)S(1)}, bf16[16,128]{1,0:T(8,128)(2,1)}, u32[]{:S(2)}) copy-start(bf16[16,128]{1,0:T(8,128)(2,1)} %get-tuple-element.8) | copy-start | bytes 12292
  97.5 35.9 %copy-start.6 = (s32[49]{0:T(128)S(1)}, s32[49]{0:T(128)}, u32[]{:S(2)}) copy-start(s32[49]{0:T(128)} %constant.41) | copy-start | bytes 592
  97.5 0.7 copy-start.2
  98.2 0.7 copy-start.3
Sparse Core Ops, SparseCore 0:
  133.4 23.9 all-gather.2

commit v2 on v1

v2 whole, which is shorter than its diff:
```python
import jax
import jax.numpy as jnp
import numpy as np
from jax import lax
from jax.experimental import pallas as pl
from jax.experimental.pallas import tpu as pltpu
from jax.sharding import PartitionSpec as P

F32 = jnp.float32
BF16 = jnp.bfloat16
I32 = jnp.int32
MESH = pl.DeviceIdType.MESH
K = 49
KP = 64
CH = 16
CP = 8
LB = 128
ATOMS = 8192
SLOTS = 189
CLASSES = 316
BOXES = 64
CHANS = 4
EMPTY = 3 * LB * CP
NT = (((1,), (1,)), ((), ()))
VMEM = pl.BlockSpec(memory_space=pltpu.VMEM)
ANY = pl.BlockSpec(memory_space=pl.ANY)
DEGREE = np.array([int(np.sqrt(k)) for k in range(K)])


def dot_nt(a, b):
    return lax.dot_general(a, b, NT, preferred_element_type=F32)


def below(block, rows):
    return jnp.concatenate([block, jnp.zeros((rows - block.shape[0], block.shape[1]), block.dtype)], 0)


def octant_tables(ref, wide):
    wide[...] = jnp.zeros_like(wide)
    wide[0 : K * 8, 0:K] = ref[...].astype(F32).reshape(K * 8, K)
    tables = []
    for o in range(8):
        part = wide[pl.ds(o, KP, stride=8), :]
        tables.append(jnp.concatenate([part, pltpu.roll(part, KP, 1)], 0).astype(BF16))
    return tables


def onehot_rows(row, count):
    shape = (count, row.shape[1])
    return jnp.where(row == lax.broadcasted_iota(I32, shape, 0), 1.0, 0.0).astype(BF16)


def far_kernel(
    feat, harm, leaf, sources, csource, cclass, up, down, transfer, ctransfer,
    out,
    hpad, acc, own32, own, before, after, mid32, wide, call, transfer_v, ctransfer_v, byrow, weights,
    index_v, index_s, table, far32, local32, picked32, source32,
    load_sem, index_sem, halo_send, halo_recv, call_send, call_recv, chan_send, chan_recv,
):
    box = lax.axis_index("box")
    chan = lax.axis_index("chan")
    load_a = pltpu.make_async_copy(transfer, transfer_v, load_sem.at[0])
    load_b = pltpu.make_async_copy(ctransfer, ctransfer_v, load_sem.at[1])
    load_a.start()
    load_b.start()
    barrier = pltpu.get_barrier_semaphore()

    def greet(d, carry):
        pl.semaphore_signal(
            barrier, inc=1, device_id={"box": lax.rem(box + d, BOXES)}, device_id_type=MESH
        )
        return carry

    lax.fori_loop(1, BOXES, greet, 0)
    for d in range(1, CHANS):
        pl.semaphore_signal(
            barrier, inc=1, device_id={"chan": lax.rem(chan + d, CHANS)}, device_id_type=MESH
        )

    step = 512
    hpad[...] = below(harm[...].astype(F32), KP).astype(BF16)
    acc[...] = jnp.zeros_like(acc)

    def turn(i, carry):
        at = pl.ds(pl.multiple_of(i * step, step), step)
        onehot = onehot_rows(leaf[:, at], LB)
        h = hpad[:, at]
        f = feat[:, at]
        for group in range(4):
            products = jnp.concatenate([h * f[4 * group + c : 4 * group + c + 1] for c in range(4)], 0)
            cols = slice(group * 256, group * 256 + 256)
            acc[:, cols] += dot_nt(onehot, products)
        return carry

    lax.fori_loop(0, ATOMS // step, turn, 0)
    for pair in range(CP):
        part = acc[:, pair * 128 : pair * 128 + 128].astype(BF16).astype(F32)
        own32[pl.ds(pair, LB, stride=CP), :] = part
    own[...] = own32[...].astype(BF16)

    pl.semaphore_wait(barrier, BOXES - 1 + CHANS - 1)
    right = {"box": lax.rem(box + 1, BOXES)}
    left = {"box": lax.rem(box + BOXES - 1, BOXES)}
    halos = [
        pltpu.make_async_remote_copy(
            src_ref=own, dst_ref=slot, send_sem=halo_send.at[i], recv_sem=halo_recv.at[i],
            device_id=where, device_id_type=MESH,
        )
        for i, (slot, where) in enumerate(((before, right), (after, left)))
    ]
    for copy in halos:
        copy.start()

    tables = octant_tables(up, wide)
    children = own32[...].reshape(16, 8, CP, 128)
    mid = jnp.zeros((128, 128), F32)
    for o in range(8):
        mid += dot_nt(children[:, o].reshape(128, 128).astype(BF16), tables[o])
    mid32[...] = mid.astype(BF16).astype(F32)
    mids = mid32[...].reshape(2, 8, CP, 128)
    coarse = jnp.zeros((16, 128), F32)
    for o in range(8):
        coarse += dot_nt(mids[:, o].reshape(16, 128).astype(BF16), tables[o])
    mine = call.at[pl.ds(pl.multiple_of(box * 16, 16), 16)]
    mine[...] = coarse.astype(BF16)

    def call_copy(d, sender):
        rows = call.at[pl.ds(pl.multiple_of(sender * 16, 16), 16)]
        return pltpu.make_async_remote_copy(
            src_ref=rows, dst_ref=rows, send_sem=call_send.at[d], recv_sem=call_recv.at[sender],
            device_id={"box": lax.rem(box + d, BOXES)}, device_id_type=MESH,
        )

    def call_start(d, carry):
        call_copy(d, box).start()
        return carry

    lax.fori_loop(1, BOXES, call_start, 0)

    rows = jnp.clip((sources[...] - (box * LB - LB)) * CP, 0, EMPTY - CP)
    rows = jnp.where(sources[...] >= 0, rows, EMPTY)
    index_rows = jnp.concatenate([rows, jnp.full((192 - SLOTS, LB), EMPTY, I32)], 0)
    quarter = lax.broadcasted_iota(I32, (8, 128), 1) // 32
    for tb in range(4):
        for jc in range(6):
            total = jnp.zeros((8, 128), I32)
            for jq in range(4):
                g = jc * 32 + jq * 8
                part = pltpu.roll(index_rows[g : g + 8], (jq - tb) % 4 * 32, 1)
                total = jnp.where(quarter == jq, part, total)
            index_v[tb * 6 + jc] = total
    index_copy = pltpu.make_async_copy(index_v, index_s, index_sem)
    index_copy.start()

    load_a.wait()
    for half in range(2):
        byrow[(half * KP + K) * 192 : (half + 1) * KP * 192, :] = jnp.zeros(((KP - K) * 192, 128), F32)
    eye = jnp.where(
        lax.broadcasted_iota(I32, (192, SLOTS), 0) == lax.broadcasted_iota(I32, (192, SLOTS), 1), 1.0, 0.0
    ).astype(BF16)

    def turn_slots(q, carry):
        block = below(transfer_v[q].astype(F32), KP).astype(BF16)
        gap = jnp.zeros((128, SLOTS), BF16)
        both = dot_nt(eye, jnp.concatenate([block, gap, block], 0))
        byrow[pl.ds(pl.multiple_of(q * 192, 192), 192), :] = both[:, :128]
        byrow[pl.ds(pl.multiple_of((KP + q) * 192, 192), 192), :] = both[:, 128:]
        return carry

    lax.fori_loop(0, K, turn_slots, 0)

    def pack_slots(i, carry):
        for r in range(4):
            j = i * 4 + r
            weights[j] = byrow[pl.ds(j, 128, stride=192), :].astype(BF16)
        return carry

    lax.fori_loop(0, 48, pack_slots, 0)

    load_b.wait()
    class_row = jnp.concatenate([cclass[0:1, :], cclass[1:2, :]], 1)
    class_hot = onehot_rows(class_row, CLASSES)

    def pick_classes(i, carry):
        blocks = [below(ctransfer_v[i * 7 + r].astype(F32), 56).astype(BF16) for r in range(7)]
        picked32[pl.ds(pl.multiple_of(i * 392, 8), 392), :] = jnp.dot(
            jnp.concatenate(blocks, 0), class_hot, preferred_element_type=F32
        )
        return carry

    lax.fori_loop(0, 7, pick_classes, 0)
    index_copy.wait()

    table[1024:2048, :] = own32[...]
    table[3072:3080, :] = jnp.zeros((8, 128), F32)
    for copy in halos:
        copy.wait()
    table[0:1024, :] = before[...].astype(F32)
    table[2048:3072, :] = after[...].astype(F32)

    def block(tb, carry):
        def chunk(jc, acc):
            def pick(jj, t):
                row = index_s[tb * 6 + jc, jj % 8, (jj // 8) * 32 + t]
                return table[pl.ds(row, 8), :]

            parts = []
            for jj in range(32):
                pairs = [
                    jnp.concatenate([pick(jj, t), pick(jj, t + 1)], 0).astype(BF16) for t in range(0, 32, 2)
                ]
                parts.append(jnp.concatenate(pairs, 0))
            lhs = jnp.concatenate(parts, 1)
            rhs = jnp.concatenate([weights[jc * 32 + jj] for jj in range(32)], 1)
            return acc + dot_nt(lhs, rhs)

        total = lax.fori_loop(0, 6, chunk, jnp.zeros((256, 128), F32))
        far32[pl.ds(pl.multiple_of(tb * 256, 256), 256), :] = total
        return carry

    def chan_copy(tb, d, sender):
        part = out.at[sender, pl.ds(pl.multiple_of(tb * 32, 32), 32)]
        return pltpu.make_async_remote_copy(
            src_ref=part, dst_ref=part, send_sem=chan_send.at[tb, d], recv_sem=chan_recv.at[tb, sender],
            device_id={"chan": lax.rem(chan + d, CHANS)}, device_id_type=MESH,
        )

    def finish(tb, carry):
        rows = pl.ds(pl.multiple_of(tb * 256, 256), 256)
        far32[rows, :] += local32[rows, :]
        for pair in range(CP):
            part = far32[pl.ds(tb * 256 + pair, 32, stride=CP), :]
            out[chan, pl.ds(pl.multiple_of(tb * 32, 32), 32), pair * 128 : pair * 128 + 128] = part.astype(BF16)
        for d in range(1, CHANS):
            chan_copy(tb, d, chan).start()
        return carry

    lax.fori_loop(0, 2, block, 0)

    def call_wait(d, carry):
        call_copy(d, box).wait_send()
        call_copy(d, lax.rem(box + BOXES - d, BOXES)).wait_recv()
        return carry

    lax.fori_loop(1, BOXES, call_wait, 0)
    source_row = jnp.concatenate([csource[0:1, :], csource[1:2, :]], 1)
    source_hot = onehot_rows(source_row, 128)
    own32[...] = call[...].astype(F32)
    for pair in range(CP):
        flat = own32[pl.ds(pair, 128, stride=CP), :].T.astype(BF16)
        source32[pair * 128 : pair * 128 + 128, :] = jnp.dot(flat, source_hot, preferred_element_type=F32)
    first_half = lax.broadcasted_iota(I32, (16, 128), 1) < KP

    def contract(i, acc):
        lhs, rhs = [], []
        for r in range(7):
            k = i * 7 + r
            rhs.append(picked32[pl.ds(k, K, stride=56), :].astype(BF16))
            both = jnp.concatenate(
                [source32[pl.ds(k, 8, stride=128), :], source32[pl.ds(KP + k, 8, stride=128), :]], 0
            )
            lhs.append(
                jnp.concatenate([jnp.where(first_half, both, 0.0), jnp.where(first_half, 0.0, both)], 0).astype(BF16)
            )
        return acc + dot_nt(jnp.concatenate(lhs, 1), jnp.concatenate(rhs, 1))

    both = lax.fori_loop(0, 7, contract, jnp.zeros((32, K), F32))
    both = jnp.concatenate([both, jnp.zeros((32, 128 - K), F32)], 1)
    coarse_local = jnp.concatenate(
        [both[0:8] + pltpu.roll(both[8:16], KP, 1), both[16:24] + pltpu.roll(both[24:32], KP, 1)], 0
    ).astype(BF16)
    tables = octant_tables(down, wide)
    for o in range(8):
        mid = dot_nt(coarse_local, tables[o])
        mid32[o * 8 : o * 8 + 8, :] = mid[:8]
        mid32[64 + o * 8 : 64 + o * 8 + 8, :] = mid[8:]
    mids = mid32[...].astype(BF16)
    for o in range(8):
        part = dot_nt(mids, tables[o])
        for m in range(16):
            local32[m * 64 + o * 8 : m * 64 + o * 8 + 8, :] = part[m * 8 : m * 8 + 8]

    lax.fori_loop(0, 2, finish, 0)

    def block_and_finish(tb, carry):
        block(tb, 0)
        finish(tb, 0)
        return carry

    lax.fori_loop(2, 4, block_and_finish, 0)

    def chan_wait(tb, carry):
        for d in range(1, CHANS):
            chan_copy(tb, d, chan).wait_send()
            chan_copy(tb, d, lax.rem(chan + CHANS - d, CHANS)).wait_recv()
        return carry

    lax.fori_loop(0, 4, chan_wait, 0)


def field_kernel(harm, leaf, local, wide_mix, out, acc, mixed):
    acc[...] = jnp.zeros_like(acc)
    for dev in range(4):
        def mix(i, carry):
            cols = pl.ds(pl.multiple_of(i * 512, 512), 512)
            weight = wide_mix[:, pl.ds(pl.multiple_of(dev * 1024 + i * 512, 512), 512)].astype(F32)
            lane = lax.rem(lax.broadcasted_iota(jnp.int32, (16, 512), 1), KP)
            lhs = jnp.concatenate([jnp.where(lane == q, weight, 0.0).astype(BF16) for q in range(K)], 0)
            acc[...] += dot_nt(lhs, local[dev, :, cols])
            return carry

        lax.fori_loop(0, 2, mix, 0)
    mixed[...] = acc[...].astype(BF16)
    step = 256

    def turn(i, carry):
        at = pl.ds(pl.multiple_of(i * step, step), step)
        onehot = jnp.where(
            leaf[:, at] == lax.broadcasted_iota(jnp.int32, (LB, step), 0), 1.0, 0.0
        ).astype(BF16)
        picked = jnp.dot(mixed[...], onehot, preferred_element_type=F32)
        h = harm[:, at].astype(F32)
        total = jnp.zeros((CH, step), F32)
        for q in range(K):
            total += h[q : q + 1] * picked[q * 16 : q * 16 + 16]
        out[:, at] = total.astype(BF16)
        return carry

    lax.fori_loop(0, ATOMS // step, turn, 0)


def on_device(
    features, harmonics, atom_leaf, leaf_sources, coarse_sources, coarse_class,
    child_to_parent, parent_to_child, leaf_transfer, coarse_transfer, mix_weight,
):
    params = dict(vmem_limit_bytes=60 << 20)
    leaf_row = atom_leaf.reshape(1, ATOMS)
    local_all = pl.pallas_call(
        far_kernel,
        out_shape=jax.ShapeDtypeStruct((CHANS, LB, 1024), BF16),
        in_specs=[VMEM] * 8 + [ANY] * 2,
        out_specs=VMEM,
        scratch_shapes=[
            pltpu.VMEM((KP, ATOMS), BF16),
            pltpu.VMEM((LB, 1024), F32),
            pltpu.VMEM((1024, 128), F32),
            pltpu.VMEM((1024, 128), BF16),
            pltpu.VMEM((1024, 128), BF16),
            pltpu.VMEM((1024, 128), BF16),
            pltpu.VMEM((128, 128), F32),
            pltpu.VMEM((KP * 8, 128), F32),
            pltpu.VMEM((BOXES * 16, 128), BF16),
            pltpu.VMEM((K, K, SLOTS), BF16),
            pltpu.VMEM((K, K, CLASSES), BF16),
            pltpu.VMEM((128 * 192, 128), F32),
            pltpu.VMEM((192, 128, 128), BF16),
            pltpu.VMEM((24, 8, 128), I32),
            pltpu.SMEM((24, 8, 128), I32),
            pltpu.VMEM((EMPTY + 8, 128), F32),
            pltpu.VMEM((1024, 128), F32),
            pltpu.VMEM((1024, 128), F32),
            pltpu.VMEM((K * 56, 128), F32),
            pltpu.VMEM((1024, 128), F32),
            pltpu.SemaphoreType.DMA((2,)),
            pltpu.SemaphoreType.DMA,
            pltpu.SemaphoreType.DMA((2,)),
            pltpu.SemaphoreType.DMA((2,)),
            pltpu.SemaphoreType.DMA((BOXES,)),
            pltpu.SemaphoreType.DMA((BOXES,)),
            pltpu.SemaphoreType.DMA((4, CHANS)),
            pltpu.SemaphoreType.DMA((4, CHANS)),
        ],
        compiler_params=pltpu.CompilerParams(collective_id=0, has_side_effects=True, **params),
        name="far",
    )(
        features, harmonics, leaf_row, leaf_sources.T, coarse_sources, coarse_class,
        child_to_parent.transpose(1, 0, 2), parent_to_child.transpose(1, 0, 2),
        leaf_transfer.transpose(1, 2, 0), coarse_transfer.transpose(1, 2, 0),
    )

    start = lax.axis_index("chan") * CH
    mine = lax.dynamic_slice_in_dim(mix_weight, start, CH, 1)
    wide = jnp.pad(mine[DEGREE], ((0, KP - K), (0, 0), (0, 0)))
    wide = wide.transpose(1, 2, 0).reshape(CH, 64 * KP)
    return pl.pallas_call(
        field_kernel,
        out_shape=jax.ShapeDtypeStruct((CH, ATOMS), BF16),
        in_specs=[VMEM] * 4,
        out_specs=VMEM,
        scratch_shapes=[pltpu.VMEM((K * 16, 128), F32), pltpu.VMEM((K * 16, 128), BF16)],
        compiler_params=pltpu.CompilerParams(**params),
        name="field",
    )(harmonics, leaf_row, local_all, wide)


def solution(mesh):
    placed = (
        P("chan", "box"), P(None, "box"), P("box"), P("box", None), P("box", None), P("box", None),
        P(), P(), P(), P(), P(),
    )
    return jax.shard_map(
        on_device, mesh=mesh, in_specs=placed, out_specs=P("chan", "box"), check_vma=False
    )
```

time: 179 us -> 91.1 us (0.51)
  blocking collectives: 51 us -> 0 us
  Pallas kernels: 59.5 us -> 88.1 us
  local copies, waits for them, and re-layouts: 24.9 us -> 2.1 us
  waiting for transfers between devices: 22.2 us -> 0 us
  between operations: 13.5 us -> 0.02 us
  starting transfers between devices: 6.84 us -> 0 us
    all_gather x1 -> x0, blocking collectives: 51 us -> none  [on_device(): coarse_all = lax.all_gather(coarse, 'box', axis=0, tiled=True)]
    pallas_call x2 -> x1, Pallas kernels: 45 us -> 73.7 us  [on_device(): pl.pallas_call(far_kernel, out_shape=jax.ShapeDtypeStruct((CHANS, LB, 102...]
    all_gather x1 -> x0, waiting for transfers between devices: 22.1 us -> none  [on_device(): local_all = lax.all_gather(local, 'chan', axis=0)]
    unnamed x22 -> x2, local copies, waits for them, and re-layouts: 20.5 us -> 0.22 us
    ppermute x2 -> x0, starting transfers between devices: 6.84 us -> none  [the longest x1 4.92 us: on_device(): before = lax.ppermute(tiles, 'box', up)]
    reshape x5 -> x0, local copies, waits for them, and re-layouts: 2.5 us -> none  [the longest x3 1.31 us: on_device(): index.reshape(4, 32, 6, 4, 8).transpose(0, 2, 4, 3, 1).reshape(24, 8, 128)]
  transfers between devices with their start and end apart: 3 -> 0, of which waited for: 1 -> 0; matrix products, arithmetic and copies ran while one was open for 13% -> 0% of each run, Pallas kernels for 0% -> 0%
where the time goes in v2:
time: 91.1 us; the launch traced here: 90.9 us
  Pallas kernels  88.1 us (97%)
  local copies, waits for them, and re-layouts  2.1 us (2%)
    pallas_call x1, Pallas kernels, on_device(): pl.pallas_call(far_kernel, out_shape=jax.ShapeDtypeStruct((CHANS, LB, 102...  73.7 us
    pallas_call x1, Pallas kernels, on_device(): pl.pallas_call(field_kernel, out_shape=jax.ShapeDtypeStruct((CH, ATOMS),...  14.5 us

profile of v2, /device:TPU:1, one launch (start us, length us, event | category | flops | bytes accessed | tf_op | source)
XLA Modules:
  0.0 90.9 jit_solution(13445947477516474160)
XLA Ops:
  0.0 0.0 copy-start
  0.0 0.7 pad_clamp_fusion
  0.7 0.2 copy-done
  0.9 0.6 gather_fusion
  1.6 0.3 copy.14
  1.9 0.9 %reshape.7.wide_mix = bf16[16,4096]{1,0:T(8,128)(2,1)} reshape(bf16[16,64,64]{2,1,0:T(8,128)(2,1)S(1)} %copy.14) | data formatting | bytes 262144 | tf_op jit(solution)/shard_map/reshape | solution.py:384
  2.8 73.7 %far.1.local = bf16[4,128,1024]{2,1,0:T(8,128)(2,1)} custom-call(bf16[16,8192]{1,0:T(8,128)(2,1)} %feat.1, bf16[49,8192]{1,0:T(8,128)(2,1)} %harm.3, s32[1,8192]{1,0:T(1,128)} %bitcast.10, s32[189,128]{1,0:T(8,128)} %bitcast.14, s32[2,64]{1,0:T(2,128)} %csource.1, s32[2,64]{1,0:T(2,128)} %cclass.1, bf16[49,8,49]{2,1,0:T(8,128)(2,1)} %bitcast.12, ...), custom_call_target="tpu_custom_call" | custom-call | tf_op jit(solution)/shard_map/far/pallas_call | solution.py:338
  76.5 14.5 %field.1 = bf16[16,8192]{1,0:T(8,128)(2,1)} custom-call(bf16[49,8192]{1,0:T(8,128)(2,1)} %harm.3, s32[1,8192]{1,0:T(1,128)} %bitcast.11, bf16[4,128,1024]{2,1,0:T(8,128)(2,1)} %far.1.local, bf16[16,4096]{1,0:T(8,128)(2,1)} %reshape.7.wide_mix), custom_call_target="tpu_custom_call" | custom-call | tf_op jit(solution)/shard_map/field/pallas_call | solution.py:385
  (2 shorter events, 0.0 us)
Async XLA Ops:
  0.0 0.9 %copy-start = (bf16[7,64,64]{2,1,0:T(8,128)(2,1)S(1)}, bf16[7,64,64]{2,1,0:T(8,128)(2,1)}, u32[]{:S(2)}) copy-start(bf16[7,64,64]{2,1,0:T(8,128)(2,1)} %param.23) | copy-start | bytes 172036

commit v3 on v2

--- a/solution.py
+++ b/solution.py
@@ -139,22 +139,13 @@
 
     rows = jnp.clip((sources[...] - (box * LB - LB)) * CP, 0, EMPTY - CP)
     rows = jnp.where(sources[...] >= 0, rows, EMPTY)
-    index_rows = jnp.concatenate([rows, jnp.full((192 - SLOTS, LB), EMPTY, I32)], 0)
-    quarter = lax.broadcasted_iota(I32, (8, 128), 1) // 32
-    for tb in range(4):
-        for jc in range(6):
-            total = jnp.zeros((8, 128), I32)
-            for jq in range(4):
-                g = jc * 32 + jq * 8
-                part = pltpu.roll(index_rows[g : g + 8], (jq - tb) % 4 * 32, 1)
-                total = jnp.where(quarter == jq, part, total)
-            index_v[tb * 6 + jc] = total
+    index_v[...] = jnp.concatenate([rows, jnp.full((192 - SLOTS, LB), EMPTY, I32)], 0)
     index_copy = pltpu.make_async_copy(index_v, index_s, index_sem)
     index_copy.start()
 
     load_a.wait()
     for half in range(2):
-        byrow[(half * KP + K) * 192 : (half + 1) * KP * 192, :] = jnp.zeros(((KP - K) * 192, 128), F32)
+        byrow[:, (half * KP + K) * 8 : (half + 1) * KP * 8, :] = jnp.zeros((24, (KP - K) * 8, 128), F32)
     eye = jnp.where(
         lax.broadcasted_iota(I32, (192, SLOTS), 0) == lax.broadcasted_iota(I32, (192, SLOTS), 1), 1.0, 0.0
     ).astype(BF16)
@@ -163,19 +154,18 @@
         block = below(transfer_v[q].astype(F32), KP).astype(BF16)
         gap = jnp.zeros((128, SLOTS), BF16)
         both = dot_nt(eye, jnp.concatenate([block, gap, block], 0))
-        byrow[pl.ds(pl.multiple_of(q * 192, 192), 192), :] = both[:, :128]
-        byrow[pl.ds(pl.multiple_of((KP + q) * 192, 192), 192), :] = both[:, 128:]
+        byrow[:, pl.ds(pl.multiple_of(q * 8, 8), 8), :] = both[:, :128].reshape(24, 8, 128)
+        byrow[:, pl.ds(pl.multiple_of((KP + q) * 8, 8), 8), :] = both[:, 128:].reshape(24, 8, 128)
         return carry
 
     lax.fori_loop(0, K, turn_slots, 0)
 
-    def pack_slots(i, carry):
-        for r in range(4):
-            j = i * 4 + r
-            weights[j] = byrow[pl.ds(j, 128, stride=192), :].astype(BF16)
-        return carry
-
-    lax.fori_loop(0, 48, pack_slots, 0)
+    def pack_slots(g, carry):
+        for r in range(8):
+            weights[g * 8 + r] = byrow[g, pl.ds(r, 128, stride=8), :].astype(BF16)
+        return carry
+
+    lax.fori_loop(0, 24, pack_slots, 0)
 
     load_b.wait()
     class_row = jnp.concatenate([cclass[0:1, :], cclass[1:2, :]], 1)
@@ -201,7 +191,7 @@
     def block(tb, carry):
         def chunk(jc, acc):
             def pick(jj, t):
-                row = index_s[tb * 6 + jc, jj % 8, (jj // 8) * 32 + t]
+                row = index_s.at[pl.ds(jj, 161), pl.ds(t, 97)][jc * 32, tb * 32]
                 return table[pl.ds(row, 8), :]
 
             parts = []
@@ -311,7 +301,7 @@
 
         lax.fori_loop(0, 2, mix, 0)
     mixed[...] = acc[...].astype(BF16)
-    step = 256
+    step = 512
 
     def turn(i, carry):
         at = pl.ds(pl.multiple_of(i * step, step), step)
@@ -352,10 +342,10 @@
             pltpu.VMEM((BOXES * 16, 128), BF16),
             pltpu.VMEM((K, K, SLOTS), BF16),
             pltpu.VMEM((K, K, CLASSES), BF16),
-            pltpu.VMEM((128 * 192, 128), F32),
+            pltpu.VMEM((24, 1024, 128), F32),
             pltpu.VMEM((192, 128, 128), BF16),
-            pltpu.VMEM((24, 8, 128), I32),
-            pltpu.SMEM((24, 8, 128), I32),
+            pltpu.VMEM((192, LB), I32),
+            pltpu.SMEM((192, LB), I32),
             pltpu.VMEM((EMPTY + 8, 128), F32),
             pltpu.VMEM((1024, 128), F32),
             pltpu.VMEM((1024, 128), F32),

time: 91.1 us -> 74.1 us (0.81)
  Pallas kernels: 88.1 us -> 71.1 us
    pallas_call x1, Pallas kernels: 73.7 us -> 60 us  [on_device(): pl.pallas_call(far_kernel, out_shape=jax.ShapeDtypeStruct((CHANS, LB, 102...]
    pallas_call x1, Pallas kernels: 14.5 us -> 11.1 us  [on_device(): pl.pallas_call(field_kernel, out_shape=jax.ShapeDtypeStruct((CH, ATOMS),...]
where the time goes in v3:
time: 74.1 us; the launch traced here: 73.9 us
  Pallas kernels  71.1 us (96%)
  local copies, waits for them, and re-layouts  2.1 us (3%)
    pallas_call x1, Pallas kernels, on_device(): pl.pallas_call(far_kernel, out_shape=jax.ShapeDtypeStruct((CHANS, LB, 102...  60 us
    pallas_call x1, Pallas kernels, on_device(): pl.pallas_call(field_kernel, out_shape=jax.ShapeDtypeStruct((CH, ATOMS),...  11.1 us

profile of v3, /device:TPU:1, one launch (start us, length us, event | category | flops | bytes accessed | tf_op | source)
XLA Modules:
  0.0 73.9 jit_solution(15566973474128939742)
XLA Ops:
  0.0 0.0 copy-start
  0.0 0.7 pad_clamp_fusion
  0.7 0.2 copy-done
  0.9 0.6 gather_fusion
  1.6 0.3 copy.14
  1.9 0.9 %reshape.7.wide_mix = bf16[16,4096]{1,0:T(8,128)(2,1)} reshape(bf16[16,64,64]{2,1,0:T(8,128)(2,1)S(1)} %copy.14) | data formatting | bytes 262144 | tf_op jit(solution)/shard_map/reshape | solution.py:374
  2.8 60.0 %far.1.local = bf16[4,128,1024]{2,1,0:T(8,128)(2,1)} custom-call(bf16[16,8192]{1,0:T(8,128)(2,1)} %feat.1, bf16[49,8192]{1,0:T(8,128)(2,1)} %harm.3, s32[1,8192]{1,0:T(1,128)} %bitcast.10, s32[189,128]{1,0:T(8,128)} %bitcast.14, s32[2,64]{1,0:T(2,128)} %csource.1, s32[2,64]{1,0:T(2,128)} %cclass.1, bf16[49,8,49]{2,1,0:T(8,128)(2,1)} %bitcast.12, ...), custom_call_target="tpu_custom_call" | custom-call | tf_op jit(solution)/shard_map/far/pallas_call | solution.py:328
  62.8 11.1 %field.1 = bf16[16,8192]{1,0:T(8,128)(2,1)} custom-call(bf16[49,8192]{1,0:T(8,128)(2,1)} %harm.3, s32[1,8192]{1,0:T(1,128)} %bitcast.11, bf16[4,128,1024]{2,1,0:T(8,128)(2,1)} %far.1.local, bf16[16,4096]{1,0:T(8,128)(2,1)} %reshape.7.wide_mix), custom_call_target="tpu_custom_call" | custom-call | tf_op jit(solution)/shard_map/field/pallas_call | solution.py:375
  (2 shorter events, 0.0 us)
Async XLA Ops:
  0.0 0.9 %copy-start = (bf16[7,64,64]{2,1,0:T(8,128)(2,1)S(1)}, bf16[7,64,64]{2,1,0:T(8,128)(2,1)}, u32[]{:S(2)}) copy-start(bf16[7,64,64]{2,1,0:T(8,128)(2,1)} %param.23) | copy-start | bytes 172036

commit v4 on v3

--- a/solution.py
+++ b/solution.py
@@ -77,7 +77,7 @@
             barrier, inc=1, device_id={"chan": lax.rem(chan + d, CHANS)}, device_id_type=MESH
         )
 
-    step = 512
+    step = 1024
     hpad[...] = below(harm[...].astype(F32), KP).astype(BF16)
     acc[...] = jnp.zeros_like(acc)
 
@@ -150,15 +150,17 @@
         lax.broadcasted_iota(I32, (192, SLOTS), 0) == lax.broadcasted_iota(I32, (192, SLOTS), 1), 1.0, 0.0
     ).astype(BF16)
 
-    def turn_slots(q, carry):
-        block = below(transfer_v[q].astype(F32), KP).astype(BF16)
+    def turn_slots(i, carry):
         gap = jnp.zeros((128, SLOTS), BF16)
-        both = dot_nt(eye, jnp.concatenate([block, gap, block], 0))
-        byrow[:, pl.ds(pl.multiple_of(q * 8, 8), 8), :] = both[:, :128].reshape(24, 8, 128)
-        byrow[:, pl.ds(pl.multiple_of((KP + q) * 8, 8), 8), :] = both[:, 128:].reshape(24, 8, 128)
-        return carry
-
-    lax.fori_loop(0, K, turn_slots, 0)
+        for r in range(7):
+            q = i * 7 + r
+            block = below(transfer_v[q].astype(F32), KP).astype(BF16)
+            both = dot_nt(eye, jnp.concatenate([block, gap, block], 0))
+            byrow[:, pl.ds(pl.multiple_of(q * 8, 8), 8), :] = both[:, :128].reshape(24, 8, 128)
+            byrow[:, pl.ds(pl.multiple_of((KP + q) * 8, 8), 8), :] = both[:, 128:].reshape(24, 8, 128)
+        return carry
+
+    lax.fori_loop(0, 7, turn_slots, 0)
 
     def pack_slots(g, carry):
         for r in range(8):
@@ -191,20 +193,20 @@
     def block(tb, carry):
         def chunk(jc, acc):
             def pick(jj, t):
-                row = index_s.at[pl.ds(jj, 161), pl.ds(t, 97)][jc * 32, tb * 32]
+                row = index_s.at[pl.ds(jj, 129), pl.ds(t, 97)][jc * 64, tb * 32]
                 return table[pl.ds(row, 8), :]
 
             parts = []
-            for jj in range(32):
+            for jj in range(64):
                 pairs = [
                     jnp.concatenate([pick(jj, t), pick(jj, t + 1)], 0).astype(BF16) for t in range(0, 32, 2)
                 ]
                 parts.append(jnp.concatenate(pairs, 0))
             lhs = jnp.concatenate(parts, 1)
-            rhs = jnp.concatenate([weights[jc * 32 + jj] for jj in range(32)], 1)
+            rhs = jnp.concatenate([weights[jc * 64 + jj] for jj in range(64)], 1)
             return acc + dot_nt(lhs, rhs)
 
-        total = lax.fori_loop(0, 6, chunk, jnp.zeros((256, 128), F32))
+        total = lax.fori_loop(0, 3, chunk, jnp.zeros((256, 128), F32))
         far32[pl.ds(pl.multiple_of(tb * 256, 256), 256), :] = total
         return carry
 

time: 74.1 us -> 63.9 us (0.86)
  Pallas kernels: 71.1 us -> 60.6 us
    pallas_call x1, Pallas kernels: 60 us -> 49.5 us  [on_device(): pl.pallas_call(far_kernel, out_shape=jax.ShapeDtypeStruct((CHANS, LB, 102...]
where the time goes in v4:
time: 63.9 us; the launch traced here: 63.5 us
  Pallas kernels  60.6 us (95%)
  local copies, waits for them, and re-layouts  2.1 us (3%)
  other arithmetic  0.69 us (1%)
    pallas_call x1, Pallas kernels, on_device(): pl.pallas_call(far_kernel, out_shape=jax.ShapeDtypeStruct((CHANS, LB, 102...  49.5 us
    pallas_call x1, Pallas kernels, on_device(): pl.pallas_call(field_kernel, out_shape=jax.ShapeDtypeStruct((CH, ATOMS),...  11.1 us

profile of v4, /device:TPU:1, one launch (start us, length us, event | category | flops | bytes accessed | tf_op | source)
XLA Modules:
  0.0 63.5 jit_solution(18275259899293056996)
XLA Ops:
  0.0 0.0 copy-start
  0.0 0.7 %pad_clamp_fusion = s32[1024]{0:T(1024)S(1)} fusion(s32[49]{0:T(128)} %constant.25), kind=kLoop, calls=%fused_computation.2 | loop fusion | flops 1024 | bytes 4292 | tf_op jit(solution)/shard_map/gather | solution.py:375
  0.7 0.2 copy-done
  0.9 0.6 gather_fusion
  1.6 0.3 copy.14
  1.9 0.9 %reshape.7.wide_mix = bf16[16,4096]{1,0:T(8,128)(2,1)} reshape(bf16[16,64,64]{2,1,0:T(8,128)(2,1)S(1)} %copy.14) | data formatting | bytes 262144 | tf_op jit(solution)/shard_map/reshape | solution.py:376
  2.8 49.5 %far.1.local = bf16[4,128,1024]{2,1,0:T(8,128)(2,1)} custom-call(bf16[16,8192]{1,0:T(8,128)(2,1)} %feat.1, bf16[49,8192]{1,0:T(8,128)(2,1)} %harm.3, s32[1,8192]{1,0:T(1,128)} %bitcast.10, s32[189,128]{1,0:T(8,128)} %bitcast.14, s32[2,64]{1,0:T(2,128)} %csource.1, s32[2,64]{1,0:T(2,128)} %cclass.1, bf16[49,8,49]{2,1,0:T(8,128)(2,1)} %bitcast.12, ...), custom_call_target="tpu_custom_call" | custom-call | tf_op jit(solution)/shard_map/far/pallas_call | solution.py:330
  52.4 11.1 %field.1 = bf16[16,8192]{1,0:T(8,128)(2,1)} custom-call(bf16[49,8192]{1,0:T(8,128)(2,1)} %harm.3, s32[1,8192]{1,0:T(1,128)} %bitcast.11, bf16[4,128,1024]{2,1,0:T(8,128)(2,1)} %far.1.local, bf16[16,4096]{1,0:T(8,128)(2,1)} %reshape.7.wide_mix), custom_call_target="tpu_custom_call" | custom-call | tf_op jit(solution)/shard_map/field/pallas_call | solution.py:377
  (2 shorter events, 0.0 us)
Async XLA Ops:
  0.0 0.9 %copy-start = (bf16[7,64,64]{2,1,0:T(8,128)(2,1)S(1)}, bf16[7,64,64]{2,1,0:T(8,128)(2,1)}, u32[]{:S(2)}) copy-start(bf16[7,64,64]{2,1,0:T(8,128)(2,1)} %param.23) | copy-start | bytes 172036

commit v5 on v4

--- a/solution.py
+++ b/solution.py
@@ -24,7 +24,8 @@
 NT = (((1,), (1,)), ((), ()))
 VMEM = pl.BlockSpec(memory_space=pltpu.VMEM)
 ANY = pl.BlockSpec(memory_space=pl.ANY)
-DEGREE = np.array([int(np.sqrt(k)) for k in range(K)])
+DEG = 7
+DEGREE = [int(np.sqrt(k)) for k in range(K)]
 
 
 def dot_nt(a, b):
@@ -51,9 +52,9 @@
 
 
 def far_kernel(
-    feat, harm, leaf, sources, csource, cclass, up, down, transfer, ctransfer,
+    feat, harm, leaf, sources, csource, cclass, up, down, mix, transfer, ctransfer,
     out,
-    hpad, acc, own32, own, before, after, mid32, wide, call, transfer_v, ctransfer_v, byrow, weights,
+    local, acc, own32, own, before, after, mid32, wide, call, transfer_v, ctransfer_v, byrow, weights,
     index_v, index_s, table, far32, local32, picked32, source32,
     load_sem, index_sem, halo_send, halo_recv, call_send, call_recv, chan_send, chan_recv,
 ):
@@ -78,24 +79,20 @@
         )
 
     step = 1024
-    hpad[...] = below(harm[...].astype(F32), KP).astype(BF16)
     acc[...] = jnp.zeros_like(acc)
 
     def turn(i, carry):
         at = pl.ds(pl.multiple_of(i * step, step), step)
-        onehot = onehot_rows(leaf[:, at], LB)
-        h = hpad[:, at]
+        h = harm[:, at]
         f = feat[:, at]
-        for group in range(4):
-            products = jnp.concatenate([h * f[4 * group + c : 4 * group + c + 1] for c in range(4)], 0)
-            cols = slice(group * 256, group * 256 + 256)
-            acc[:, cols] += dot_nt(onehot, products)
+        products = jnp.concatenate([h[k : k + 1] * f for k in range(K)], 0)
+        acc[0 : K * CH, :] += dot_nt(products, onehot_rows(leaf[:, at], LB))
         return carry
 
     lax.fori_loop(0, ATOMS // step, turn, 0)
     for pair in range(CP):
-        part = acc[:, pair * 128 : pair * 128 + 128].astype(BF16).astype(F32)
-        own32[pl.ds(pair, LB, stride=CP), :] = part
+        both = jnp.concatenate([acc[pl.ds(2 * pair + p, KP, stride=CH), :] for p in range(2)], 0)
+        own32[pl.ds(pair, LB, stride=CP), :] = both.T.astype(BF16).astype(F32)
     own[...] = own32[...].astype(BF16)
 
     pl.semaphore_wait(barrier, BOXES - 1 + CHANS - 1)
@@ -190,28 +187,27 @@
     table[0:1024, :] = before[...].astype(F32)
     table[2048:3072, :] = after[...].astype(F32)
 
-    def block(tb, carry):
+    def block(width, slots, tb):
         def chunk(jc, acc):
             def pick(jj, t):
-                row = index_s.at[pl.ds(jj, 129), pl.ds(t, 97)][jc * 64, tb * 32]
-                return table[pl.ds(row, 8), :]
+                start = index_s.at[pl.ds(jj, 193 - slots), pl.ds(t, LB + 1 - width)]
+                return table[pl.ds(start[jc * slots, tb * width], 8), :]
 
             parts = []
-            for jj in range(64):
+            for jj in range(slots):
                 pairs = [
-                    jnp.concatenate([pick(jj, t), pick(jj, t + 1)], 0).astype(BF16) for t in range(0, 32, 2)
+                    jnp.concatenate([pick(jj, t), pick(jj, t + 1)], 0).astype(BF16) for t in range(0, width, 2)
                 ]
                 parts.append(jnp.concatenate(pairs, 0))
             lhs = jnp.concatenate(parts, 1)
-            rhs = jnp.concatenate([weights[jc * 64 + jj] for jj in range(64)], 1)
+            rhs = jnp.concatenate([weights[jc * slots + jj] for jj in range(slots)], 1)
             return acc + dot_nt(lhs, rhs)
 
-        total = lax.fori_loop(0, 3, chunk, jnp.zeros((256, 128), F32))
-        far32[pl.ds(pl.multiple_of(tb * 256, 256), 256), :] = total
-        return carry
+        total = lax.fori_loop(0, 192 // slots, chunk, jnp.zeros((width * CP, 128), F32))
+        far32[pl.ds(pl.multiple_of(tb * width * CP, width * CP), width * CP), :] = total
 
     def chan_copy(tb, d, sender):
-        part = out.at[sender, pl.ds(pl.multiple_of(tb * 32, 32), 32)]
+        part = local.at[sender, pl.ds(pl.multiple_of(tb * 32, 32), 32)]
         return pltpu.make_async_remote_copy(
             src_ref=part, dst_ref=part, send_sem=chan_send.at[tb, d], recv_sem=chan_recv.at[tb, sender],
             device_id={"chan": lax.rem(chan + d, CHANS)}, device_id_type=MESH,
@@ -222,12 +218,12 @@
         far32[rows, :] += local32[rows, :]
         for pair in range(CP):
             part = far32[pl.ds(tb * 256 + pair, 32, stride=CP), :]
-            out[chan, pl.ds(pl.multiple_of(tb * 32, 32), 32), pair * 128 : pair * 128 + 128] = part.astype(BF16)
-        for d in range(1, CHANS):
+            local[chan, pl.ds(pl.multiple_of(tb * 32, 32), 32), pair * 128 : pair * 128 + 128] = part.astype(BF16)
+        for d in (3, 1, 2):
             chan_copy(tb, d, chan).start()
         return carry
 
-    lax.fori_loop(0, 2, block, 0)
+    block(64, 32, 0)
 
     def call_wait(d, carry):
         call_copy(d, box).wait_send()
@@ -275,46 +271,58 @@
     lax.fori_loop(0, 2, finish, 0)
 
     def block_and_finish(tb, carry):
-        block(tb, 0)
+        block(32, 64, tb)
         finish(tb, 0)
         return carry
 
     lax.fori_loop(2, 4, block_and_finish, 0)
+
+    mine = pl.ds(pl.multiple_of(chan * CH, CH), CH)
+    mixes = jnp.concatenate([mix[l, mine, :] for l in range(DEG)], 0)
+    lane = lax.broadcasted_iota(I32, (CH, 512), 1) % KP
+    ahead = lax.broadcasted_iota(I32, (64, 512), 0) - lax.broadcasted_iota(I32, (64, 512), 1) // KP
+    mixed = acc.at[0 : K * CH]
+    mixed[...] = jnp.zeros((K * CH, LB), F32)
+    for d in (0, 3, 1, 2):
+        sender = lax.rem(chan + CHANS - d, CHANS)
+        if d:
+            for tb in range(4):
+                chan_copy(tb, d, sender).wait_recv()
+
+        def blend(i, carry):
+            spread = jnp.where(ahead == sender * CH + i * 8, 1.0, 0.0).astype(BF16)
+            weight = jnp.dot(mixes, spread, preferred_element_type=F32)
+            lhs = jnp.concatenate(
+                [
+                    jnp.where(lane == k, weight[CH * DEGREE[k] : CH * DEGREE[k] + CH], 0.0).astype(BF16)
+                    for k in range(K)
+                ],
+                0,
+            )
+            mixed[...] += dot_nt(lhs, local[sender, :, pl.ds(pl.multiple_of(i * 512, 512), 512)])
+            return carry
+
+        lax.fori_loop(0, 2, blend, 0)
+    out[...] = mixed[...].astype(BF16)
 
     def chan_wait(tb, carry):
         for d in range(1, CHANS):
             chan_copy(tb, d, chan).wait_send()
-            chan_copy(tb, d, lax.rem(chan + CHANS - d, CHANS)).wait_recv()
         return carry
 
     lax.fori_loop(0, 4, chan_wait, 0)
 
 
-def field_kernel(harm, leaf, local, wide_mix, out, acc, mixed):
-    acc[...] = jnp.zeros_like(acc)
-    for dev in range(4):
-        def mix(i, carry):
-            cols = pl.ds(pl.multiple_of(i * 512, 512), 512)
-            weight = wide_mix[:, pl.ds(pl.multiple_of(dev * 1024 + i * 512, 512), 512)].astype(F32)
-            lane = lax.rem(lax.broadcasted_iota(jnp.int32, (16, 512), 1), KP)
-            lhs = jnp.concatenate([jnp.where(lane == q, weight, 0.0).astype(BF16) for q in range(K)], 0)
-            acc[...] += dot_nt(lhs, local[dev, :, cols])
-            return carry
-
-        lax.fori_loop(0, 2, mix, 0)
-    mixed[...] = acc[...].astype(BF16)
-    step = 512
+def field_kernel(harm, leaf, mixed, out):
+    step = 1024
 
     def turn(i, carry):
         at = pl.ds(pl.multiple_of(i * step, step), step)
-        onehot = jnp.where(
-            leaf[:, at] == lax.broadcasted_iota(jnp.int32, (LB, step), 0), 1.0, 0.0
-        ).astype(BF16)
-        picked = jnp.dot(mixed[...], onehot, preferred_element_type=F32)
+        picked = jnp.dot(mixed[...], onehot_rows(leaf[:, at], LB), preferred_element_type=F32)
         h = harm[:, at].astype(F32)
         total = jnp.zeros((CH, step), F32)
-        for q in range(K):
-            total += h[q : q + 1] * picked[q * 16 : q * 16 + 16]
+        for k in range(K):
+            total += h[k : k + 1] * picked[k * CH : k * CH + CH]
         out[:, at] = total.astype(BF16)
         return carry
 
@@ -327,14 +335,14 @@
 ):
     params = dict(vmem_limit_bytes=60 << 20)
     leaf_row = atom_leaf.reshape(1, ATOMS)
-    local_all = pl.pallas_call(
+    mixed = pl.pallas_call(
         far_kernel,
-        out_shape=jax.ShapeDtypeStruct((CHANS, LB, 1024), BF16),
-        in_specs=[VMEM] * 8 + [ANY] * 2,
+        out_shape=jax.ShapeDtypeStruct((K * CH, LB), BF16),
+        in_specs=[VMEM] * 9 + [ANY] * 2,
         out_specs=VMEM,
         scratch_shapes=[
-            pltpu.VMEM((KP, ATOMS), BF16),
-            pltpu.VMEM((LB, 1024), F32),
+            pltpu.VMEM((CHANS, LB, 1024), BF16),
+            pltpu.VMEM((KP * CH, LB), F32),
             pltpu.VMEM((1024, 128), F32),
             pltpu.VMEM((1024, 128), BF16),
             pltpu.VMEM((1024, 128), BF16),
@@ -366,23 +374,18 @@
         name="far",
     )(
         features, harmonics, leaf_row, leaf_sources.T, coarse_sources, coarse_class,
-        child_to_parent.transpose(1, 0, 2), parent_to_child.transpose(1, 0, 2),
+        child_to_parent.transpose(1, 0, 2), parent_to_child.transpose(1, 0, 2), mix_weight,
         leaf_transfer.transpose(1, 2, 0), coarse_transfer.transpose(1, 2, 0),
     )
 
-    start = lax.axis_index("chan") * CH
-    mine = lax.dynamic_slice_in_dim(mix_weight, start, CH, 1)
-    wide = jnp.pad(mine[DEGREE], ((0, KP - K), (0, 0), (0, 0)))
-    wide = wide.transpose(1, 2, 0).reshape(CH, 64 * KP)
     return pl.pallas_call(
         field_kernel,
         out_shape=jax.ShapeDtypeStruct((CH, ATOMS), BF16),
-        in_specs=[VMEM] * 4,
+        in_specs=[VMEM] * 3,
         out_specs=VMEM,
-        scratch_shapes=[pltpu.VMEM((K * 16, 128), F32), pltpu.VMEM((K * 16, 128), BF16)],
         compiler_params=pltpu.CompilerParams(**params),
         name="field",
-    )(harmonics, leaf_row, local_all, wide)
+    )(harmonics, leaf_row, mixed)
 
 
 def solution(mesh):

time: 63.9 us -> 57.6 us (0.901)
  Pallas kernels: 60.6 us -> 57.1 us
  local copies, waits for them, and re-layouts: 2.1 us -> 0 us
  other arithmetic: 0.69 us -> 0 us
    pallas_call x1, Pallas kernels: 11.1 us -> 6.51 us  [on_device(): pl.pallas_call(field_kernel, out_shape=jax.ShapeDtypeStruct((CH, ATOMS),...]
    pallas_call x1, Pallas kernels: 49.5 us -> 50.6 us  [on_device(): pl.pallas_call(far_kernel, out_shape=jax.ShapeDtypeStruct((K * CH, LB), B...]
    reshape x1 -> x0, local copies, waits for them, and re-layouts: 0.93 us -> none  [on_device(): wide = wide.transpose(1, 2, 0).reshape(CH, 64 * KP)]
    gather x1 -> x0, other arithmetic: 0.69 us -> none  [on_device(): wide = jnp.pad(mine[DEGREE], ((0, KP - K), (0, 0), (0, 0)))]
where the time goes in v5:
time: 57.6 us; the launch traced here: 57.2 us
  Pallas kernels  57.1 us (99%)
    pallas_call x1, Pallas kernels, on_device(): pl.pallas_call(far_kernel, out_shape=jax.ShapeDtypeStruct((K * CH, LB), B...  50.6 us
    pallas_call x1, Pallas kernels, on_device(): pl.pallas_call(field_kernel, out_shape=jax.ShapeDtypeStruct((CH, ATOMS),...  6.51 us

profile of v5, /device:TPU:1, one launch (start us, length us, event | category | flops | bytes accessed | tf_op | source)
XLA Modules:
  0.0 57.2 jit_solution(5988382856424529902)
XLA Ops:
  0.0 50.6 %far.1.mixed = bf16[784,128]{1,0:T(8,128)(2,1)} custom-call(bf16[16,8192]{1,0:T(8,128)(2,1)} %feat.1, bf16[49,8192]{1,0:T(8,128)(2,1)} %harm.3, s32[1,8192]{1,0:T(1,128)} %bitcast.8, s32[189,128]{1,0:T(8,128)} %bitcast.12, s32[2,64]{1,0:T(2,128)} %csource.1, s32[2,64]{1,0:T(2,128)} %cclass.1, bf16[49,8,49]{2,1,0:T(8,128)(2,1)} %bitcast.10, ...), custom_call_target="tpu_custom_call" | custom-call | tf_op jit(solution)/shard_map/far/pallas_call | solution.py:338
  50.6 6.5 %field.1 = bf16[16,8192]{1,0:T(8,128)(2,1)} custom-call(bf16[49,8192]{1,0:T(8,128)(2,1)} %harm.3, s32[1,8192]{1,0:T(1,128)} %bitcast.9, bf16[784,128]{1,0:T(8,128)(2,1)} %far.1.mixed), custom_call_target="tpu_custom_call" | custom-call | tf_op jit(solution)/shard_map/field/pallas_call | solution.py:381

commit v6 on v5

--- a/solution.py
+++ b/solution.py
@@ -19,6 +19,8 @@
 SLOTS = 189
 CLASSES = 316
 BOXES = 64
+GROUP = 16
+PLANES = 4
 CHANS = 4
 EMPTY = 3 * LB * CP
 NT = (((1,), (1,)), ((), ()))
@@ -56,7 +58,7 @@
     out,
     local, acc, own32, own, before, after, mid32, wide, call, transfer_v, ctransfer_v, byrow, weights,
     index_v, index_s, table, far32, local32, picked32, source32,
-    load_sem, index_sem, halo_send, halo_recv, call_send, call_recv, chan_send, chan_recv,
+    load_sem, index_sem, halo_send, halo_recv, call_send, call_recv, plane_send, plane_recv, chan_send, chan_recv,
 ):
     box = lax.axis_index("box")
     chan = lax.axis_index("chan")
@@ -66,17 +68,27 @@
     load_b.start()
     barrier = pltpu.get_barrier_semaphore()
 
+    ring = lax.rem(box, GROUP)
+    plane = box - ring
+
+    def beside(d):
+        return {"box": plane + lax.rem(ring + d, GROUP)}
+
+    def across(e):
+        return {"box": lax.rem(box + e * GROUP, BOXES)}
+
+    right = {"box": lax.rem(box + 1, BOXES)}
+    left = {"box": lax.rem(box + BOXES - 1, BOXES)}
+
     def greet(d, carry):
-        pl.semaphore_signal(
-            barrier, inc=1, device_id={"box": lax.rem(box + d, BOXES)}, device_id_type=MESH
-        )
-        return carry
-
-    lax.fori_loop(1, BOXES, greet, 0)
-    for d in range(1, CHANS):
-        pl.semaphore_signal(
-            barrier, inc=1, device_id={"chan": lax.rem(chan + d, CHANS)}, device_id_type=MESH
-        )
+        pl.semaphore_signal(barrier, inc=1, device_id=beside(d), device_id_type=MESH)
+        return carry
+
+    lax.fori_loop(1, GROUP, greet, 0)
+    others = [right, left] + [across(e) for e in range(1, PLANES)]
+    others += [{"chan": lax.rem(chan + d, CHANS)} for d in range(1, CHANS)]
+    for where in others:
+        pl.semaphore_signal(barrier, inc=1, device_id=where, device_id_type=MESH)
 
     step = 1024
     acc[...] = jnp.zeros_like(acc)
@@ -95,9 +107,7 @@
         own32[pl.ds(pair, LB, stride=CP), :] = both.T.astype(BF16).astype(F32)
     own[...] = own32[...].astype(BF16)
 
-    pl.semaphore_wait(barrier, BOXES - 1 + CHANS - 1)
-    right = {"box": lax.rem(box + 1, BOXES)}
-    left = {"box": lax.rem(box + BOXES - 1, BOXES)}
+    pl.semaphore_wait(barrier, GROUP - 1 + len(others))
     halos = [
         pltpu.make_async_remote_copy(
             src_ref=own, dst_ref=slot, send_sem=halo_send.at[i], recv_sem=halo_recv.at[i],
@@ -122,17 +132,25 @@
     mine[...] = coarse.astype(BF16)
 
     def call_copy(d, sender):
-        rows = call.at[pl.ds(pl.multiple_of(sender * 16, 16), 16)]
+        rows = call.at[pl.ds(pl.multiple_of((plane + sender) * 16, 16), 16)]
         return pltpu.make_async_remote_copy(
             src_ref=rows, dst_ref=rows, send_sem=call_send.at[d], recv_sem=call_recv.at[sender],
-            device_id={"box": lax.rem(box + d, BOXES)}, device_id_type=MESH,
+            device_id=beside(d), device_id_type=MESH,
         )
 
+    def plane_copy(e, sender):
+        rows = call.at[pl.ds(pl.multiple_of(sender * 16, 256), 256)]
+        slot = lax.div(sender, GROUP)
+        return pltpu.make_async_remote_copy(
+            src_ref=rows, dst_ref=rows, send_sem=plane_send.at[e], recv_sem=plane_recv.at[slot],
+            device_id=across(e), device_id_type=MESH,
+        )
+
     def call_start(d, carry):
-        call_copy(d, box).start()
-        return carry
-
-    lax.fori_loop(1, BOXES, call_start, 0)
+        call_copy(d, ring).start()
+        return carry
+
+    lax.fori_loop(1, GROUP, call_start, 0)
 
     rows = jnp.clip((sources[...] - (box * LB - LB)) * CP, 0, EMPTY - CP)
     rows = jnp.where(sources[...] >= 0, rows, EMPTY)
@@ -182,6 +200,15 @@
 
     table[1024:2048, :] = own32[...]
     table[3072:3080, :] = jnp.zeros((8, 128), F32)
+
+    def call_wait(d, carry):
+        call_copy(d, ring).wait_send()
+        call_copy(d, lax.rem(ring + GROUP - d, GROUP)).wait_recv()
+        return carry
+
+    lax.fori_loop(1, GROUP, call_wait, 0)
+    for e in range(1, PLANES):
+        plane_copy(e, plane).start()
     for copy in halos:
         copy.wait()
     table[0:1024, :] = before[...].astype(F32)
@@ -225,12 +252,9 @@
 
     block(64, 32, 0)
 
-    def call_wait(d, carry):
-        call_copy(d, box).wait_send()
-        call_copy(d, lax.rem(box + BOXES - d, BOXES)).wait_recv()
-        return carry
-
-    lax.fori_loop(1, BOXES, call_wait, 0)
+    for e in range(1, PLANES):
+        plane_copy(e, plane).wait_send()
+        plane_copy(e, lax.rem(plane + BOXES - e * GROUP, BOXES)).wait_recv()
     source_row = jnp.concatenate([csource[0:1, :], csource[1:2, :]], 1)
     source_hot = onehot_rows(source_row, 128)
     own32[...] = call[...].astype(F32)
@@ -365,8 +389,10 @@
             pltpu.SemaphoreType.DMA,
             pltpu.SemaphoreType.DMA((2,)),
             pltpu.SemaphoreType.DMA((2,)),
-            pltpu.SemaphoreType.DMA((BOXES,)),
-            pltpu.SemaphoreType.DMA((BOXES,)),
+            pltpu.SemaphoreType.DMA((GROUP,)),
+            pltpu.SemaphoreType.DMA((GROUP,)),
+            pltpu.SemaphoreType.DMA((PLANES,)),
+            pltpu.SemaphoreType.DMA((PLANES,)),
             pltpu.SemaphoreType.DMA((4, CHANS)),
             pltpu.SemaphoreType.DMA((4, CHANS)),
         ],

time: 57.6 us -> 53.8 us (0.934)
  Pallas kernels: 57.1 us -> 53.7 us
    pallas_call x1, Pallas kernels: 50.6 us -> 47.2 us  [on_device(): pl.pallas_call(far_kernel, out_shape=jax.ShapeDtypeStruct((K * CH, LB), B...]
where the time goes in v6:
time: 53.8 us; the launch traced here: 53.7 us
  Pallas kernels  53.7 us (100%)
    pallas_call x1, Pallas kernels, on_device(): pl.pallas_call(far_kernel, out_shape=jax.ShapeDtypeStruct((K * CH, LB), B...  47.2 us
    pallas_call x1, Pallas kernels, on_device(): pl.pallas_call(field_kernel, out_shape=jax.ShapeDtypeStruct((CH, ATOMS),...  6.51 us

profile of v6, /device:TPU:1, one launch (start us, length us, event | category | flops | bytes accessed | tf_op | source)
XLA Modules:
  0.0 53.7 jit_solution(11629660636045959705)
XLA Ops:
  0.0 47.2 %far.1.mixed = bf16[784,128]{1,0:T(8,128)(2,1)} custom-call(bf16[16,8192]{1,0:T(8,128)(2,1)} %feat.1, bf16[49,8192]{1,0:T(8,128)(2,1)} %harm.3, s32[1,8192]{1,0:T(1,128)} %bitcast.8, s32[189,128]{1,0:T(8,128)} %bitcast.12, s32[2,64]{1,0:T(2,128)} %csource.1, s32[2,64]{1,0:T(2,128)} %cclass.1, bf16[49,8,49]{2,1,0:T(8,128)(2,1)} %bitcast.10, ...), custom_call_target="tpu_custom_call" | custom-call | tf_op jit(solution)/shard_map/far/pallas_call | solution.py:362
  47.2 6.5 %field.1 = bf16[16,8192]{1,0:T(8,128)(2,1)} custom-call(bf16[49,8192]{1,0:T(8,128)(2,1)} %harm.3, s32[1,8192]{1,0:T(1,128)} %bitcast.9, bf16[784,128]{1,0:T(8,128)(2,1)} %far.1.mixed), custom_call_target="tpu_custom_call" | custom-call | tf_op jit(solution)/shard_map/field/pallas_call | solution.py:407

commit v7 on v6

--- a/solution.py
+++ b/solution.py
@@ -56,7 +56,7 @@
 def far_kernel(
     feat, harm, leaf, sources, csource, cclass, up, down, mix, transfer, ctransfer,
     out,
-    local, acc, own32, own, before, after, mid32, wide, call, transfer_v, ctransfer_v, byrow, weights,
+    local, mixed16, acc, own32, own, before, after, mid32, wide, call, transfer_v, ctransfer_v, byrow, weights,
     index_v, index_s, table, far32, local32, picked32, source32,
     load_sem, index_sem, halo_send, halo_recv, call_send, call_recv, plane_send, plane_recv, chan_send, chan_recv,
 ):
@@ -327,22 +327,11 @@
             return carry
 
         lax.fori_loop(0, 2, blend, 0)
-    out[...] = mixed[...].astype(BF16)
-
-    def chan_wait(tb, carry):
-        for d in range(1, CHANS):
-            chan_copy(tb, d, chan).wait_send()
-        return carry
-
-    lax.fori_loop(0, 4, chan_wait, 0)
-
-
-def field_kernel(harm, leaf, mixed, out):
-    step = 1024
-
-    def turn(i, carry):
+    mixed16[...] = mixed[...].astype(BF16)
+
+    def evaluate(i, carry):
         at = pl.ds(pl.multiple_of(i * step, step), step)
-        picked = jnp.dot(mixed[...], onehot_rows(leaf[:, at], LB), preferred_element_type=F32)
+        picked = jnp.dot(mixed16[...], onehot_rows(leaf[:, at], LB), preferred_element_type=F32)
         h = harm[:, at].astype(F32)
         total = jnp.zeros((CH, step), F32)
         for k in range(K):
@@ -350,7 +339,14 @@
         out[:, at] = total.astype(BF16)
         return carry
 
-    lax.fori_loop(0, ATOMS // step, turn, 0)
+    lax.fori_loop(0, ATOMS // step, evaluate, 0)
+
+    def chan_wait(tb, carry):
+        for d in range(1, CHANS):
+            chan_copy(tb, d, chan).wait_send()
+        return carry
+
+    lax.fori_loop(0, 4, chan_wait, 0)
 
 
 def on_device(
@@ -359,13 +355,14 @@
 ):
     params = dict(vmem_limit_bytes=60 << 20)
     leaf_row = atom_leaf.reshape(1, ATOMS)
-    mixed = pl.pallas_call(
+    return pl.pallas_call(
         far_kernel,
-        out_shape=jax.ShapeDtypeStruct((K * CH, LB), BF16),
+        out_shape=jax.ShapeDtypeStruct((CH, ATOMS), BF16),
         in_specs=[VMEM] * 9 + [ANY] * 2,
         out_specs=VMEM,
         scratch_shapes=[
             pltpu.VMEM((CHANS, LB, 1024), BF16),
+            pltpu.VMEM((K * CH, LB), BF16),
             pltpu.VMEM((KP * CH, LB), F32),
             pltpu.VMEM((1024, 128), F32),
             pltpu.VMEM((1024, 128), BF16),
@@ -404,15 +401,6 @@
         leaf_transfer.transpose(1, 2, 0), coarse_transfer.transpose(1, 2, 0),
     )
 
-    return pl.pallas_call(
-        field_kernel,
-        out_shape=jax.ShapeDtypeStruct((CH, ATOMS), BF16),
-        in_specs=[VMEM] * 3,
-        out_specs=VMEM,
-        compiler_params=pltpu.CompilerParams(**params),
-        name="field",
-    )(harmonics, leaf_row, mixed)
-
 
 def solution(mesh):
     placed = (

time: 53.8 us -> 53.6 us (level)
  Pallas kernels: 53.7 us -> 51.8 us
  local copies, waits for them, and re-layouts: 0 us -> 1.67 us
    pallas_call x2 -> x1, Pallas kernels: 53.7 us -> 51.8 us  [on_device(): pl.pallas_call(far_kernel, out_shape=jax.ShapeDtypeStruct((CH, ATOMS), BF...]
    unnamed x0 -> x1, local copies, waits for them, and re-layouts: none -> 1.67 us
where the time goes in v7:
time: 53.6 us; the launch traced here: 53.5 us
  Pallas kernels  51.8 us (97%)
  local copies, waits for them, and re-layouts  1.67 us (3%)
    pallas_call x1, Pallas kernels, on_device(): pl.pallas_call(far_kernel, out_shape=jax.ShapeDtypeStruct((CH, ATOMS), BF...  51.8 us
    unnamed x1, local copies, waits for them, and re-layouts  1.67 us

profile of v7, /device:TPU:1, one launch (start us, length us, event | category | flops | bytes accessed | tf_op | source)
XLA Modules:
  0.0 53.5 jit_solution(15965884793551518996)
XLA Ops:
  0.0 51.8 %far.1 = bf16[16,8192]{1,0:T(8,128)(2,1)} custom-call(bf16[16,8192]{1,0:T(8,128)(2,1)} %feat.1, bf16[49,8192]{1,0:T(8,128)(2,1)} %harm.1, s32[1,8192]{1,0:T(1,128)} %bitcast.11, s32[189,128]{1,0:T(8,128)} %bitcast.10, s32[2,64]{1,0:T(2,128)} %csource.1, s32[2,64]{1,0:T(2,128)} %cclass.1, bf16[49,8,49]{2,1,0:T(8,128)(2,1)} %bitcast.8, ...), custom_call_target="tpu_custom_call" | custom-call | tf_op jit(solution)/shard_map/far/pallas_call | solution.py:358
  51.8 1.7 %copy.13 = bf16[16,8192]{1,0:T(8,128)(2,1)} copy(bf16[16,8192]{1,0:T(8,128)(2,1)} %far.1) | data formatting | bytes 524288
